TPU v7x, 256 devices: a whole 4x4x8 slice. The times are simulated.
256 devices in a mesh: blk: 64 (over z, y_hi, x), grp: 4 (over y_lo, core).
Axes of the slice: x: 4, y: 4 (y_hi: 2, y_lo: 2; y = y_hi * 2 + y_lo), z: 8, core: 2. Of those that a mesh axis runs over, the one named last changes fastest.
Arguments:
- image_embed: bfloat16 [4, 8192, 1024], P('grp', 'blk'), may hold values from -2 to 2, as said below
- text_embed: bfloat16 [4, 8192, 1024], P('grp', 'blk'), may hold values from -2 to 2
- logit_scale: float32 [], replicated, may hold values from 30 to 100
- block_input: bfloat16 [256, 7, 7, 3072], P(('blk', 'grp')), may hold values from -6 to 6
- dw_kernel: bfloat16 [7, 7, 3072], replicated, may hold values from -0.875 to 0.875
- dw_bias: bfloat16 [3072], replicated, may hold values from -0.5 to 0.5
- ln_gain: bfloat16 [3072], replicated, may hold values from 0.5 to 1.5
- block_grad: bfloat16 [256, 7, 7, 3072], P(('blk', 'grp')), may hold values from -6 to 6
Outputs:
- image_grad: bfloat16 [4, 8192, 1024], P('grp', 'blk')
- text_grad: bfloat16 [4, 8192, 1024], P('grp', 'blk')
- input_grad: bfloat16 [256, 7, 7, 3072], P(('blk', 'grp'))
- kernel_grad: float32 [7, 7, 3072], replicated
- channel_grads: float32 [3, 3072], replicated
Inputs may be any that keep to these rules, and one draw needn't show every extreme that they name: `image_embed`: every row is nonzero.
All inputs are finite; a program needn't handle non-finite values.
Results may differ from a plain program's by a relative error of at most 0.0079.
Values may be sent and summed in bfloat16 or wider, within the bound.
A program may use at most 128 MiB of HBM per device.

v0:
```python
import jax
import jax.numpy as jnp
from jax import lax
from jax.sharding import PartitionSpec as P

GRID = 7
KS = 7


EPS = 1e-06


def joined(value, axis, join):
    pieces = jax.tree.map(lambda part: lax.all_gather(part, axis), value)
    head = jax.tree.map(lambda part: part[0], pieces)
    tail = jax.tree.map(lambda part: part[1:], pieces)
    subtotal, _ = lax.scan(lambda subtotal, section: (join(subtotal, section), None), head, tail)
    return subtotal


def normalize(raw):
    values = raw.astype(jnp.float32)
    inverse = lax.rsqrt(jnp.sum(values * values, axis=-1, keepdims=True) + EPS)
    return (values * inverse, inverse)


def project_back(grad_hat, unit_hat, inverse):
    along = jnp.sum(grad_hat * unit_hat, axis=-1, keepdims=True)
    return inverse * (grad_hat - along * unit_hat)


def log_sum_exp(logits, axis):
    peak = jnp.max(logits, axis=axis, keepdims=True)
    return jnp.squeeze(peak, axis) + jnp.log(jnp.sum(jnp.exp(logits - peak), axis=axis))


def contract_last(left_side, right_side):
    return lax.dot_general(
        left_side, right_side, (((1,), (1,)), ((), ())), preferred_element_type=jnp.float32
    )


def contract_first(left_side, right_side):
    return lax.dot_general(
        left_side, right_side, (((0,), (0,)), ((), ())), preferred_element_type=jnp.float32
    )


def combine_stats(left_pair, right_pair):
    peak = jnp.maximum(left_pair[0], right_pair[0])
    mass = left_pair[1] * jnp.exp(left_pair[0] - peak) + right_pair[1] * jnp.exp(
        right_pair[0] - peak
    )
    return (peak, mass)


def block_terms(image, upstream, kernel, bias, gain):
    edge = KS // 2
    padded = jnp.pad(image.astype(jnp.float32), ((edge, edge), (edge, edge), (0, 0)))
    kernel_f = kernel.astype(jnp.float32)
    conv_out = jnp.zeros(image.shape, jnp.float32) + bias.astype(jnp.float32)
    for tap_row in range(KS):
        for tap_col in range(KS):
            conv_out = (
                conv_out
                + padded[tap_row : tap_row + GRID, tap_col : tap_col + GRID]
                * kernel_f[tap_row, tap_col]
            )
    centre = conv_out - jnp.mean(conv_out, axis=-1, keepdims=True)
    inv_std = lax.rsqrt(jnp.mean(centre * centre, axis=-1, keepdims=True) + EPS)
    normed = centre * inv_std
    upstream_f = upstream.astype(jnp.float32)
    d_normed = upstream_f * gain.astype(jnp.float32)
    d_conv = inv_std * (
        d_normed
        - jnp.mean(d_normed, axis=-1, keepdims=True)
        - normed * jnp.mean(d_normed * normed, axis=-1, keepdims=True)
    )
    kernel_term = jnp.stack(
        [
            jnp.sum(
                d_conv * padded[tap_row : tap_row + GRID, tap_col : tap_col + GRID], axis=(0, 1)
            )
            for tap_row in range(KS)
            for tap_col in range(KS)
        ]
    )
    d_padded = jnp.pad(d_conv, ((edge, edge), (edge, edge), (0, 0)))
    d_input = jnp.zeros(image.shape, jnp.float32)
    for tap_row in range(KS):
        for tap_col in range(KS):
            start_row = KS - 1 - tap_row
            start_col = KS - 1 - tap_col
            d_input = (
                d_input
                + d_padded[start_row : start_row + GRID, start_col : start_col + GRID]
                * kernel_f[tap_row, tap_col]
            )
    channel_term = jnp.stack(
        [
            jnp.sum(d_conv, axis=(0, 1)),
            jnp.sum(upstream_f * normed, axis=(0, 1)),
            jnp.sum(upstream_f, axis=(0, 1)),
        ]
    )
    return (d_input.astype(jnp.bfloat16), jnp.concatenate([kernel_term, channel_term], axis=0))


def per_device(
    image_embed, text_embed, logit_scale, block_input, dw_kernel, dw_bias, ln_gain, block_grad
):
    d_input, terms = block_terms(block_input[0], block_grad[0], dw_kernel, dw_bias, ln_gain)
    totals = lax.psum(terms, ("blk", "grp"))
    totals = totals / (lax.axis_size("blk") * lax.axis_size("grp"))
    kernel_grad = totals[: KS * KS].reshape(KS, KS, totals.shape[1])
    channel_grads = totals[KS * KS :]
    unit_image, inv_image = normalize(image_embed[0])
    unit_text, inv_text = normalize(text_embed[0])
    hat_image = unit_image.astype(jnp.bfloat16)
    hat_text = unit_text.astype(jnp.bfloat16)
    all_texts = lax.all_gather(hat_text, "blk", axis=0, tiled=True)
    logits = contract_last(hat_image, all_texts) * logit_scale
    row_lse = log_sum_exp(logits, 1)
    col_peak = jnp.max(logits, axis=0)
    col_mass = jnp.sum(jnp.exp(logits - col_peak[None, :]), axis=0)
    peak_all, mass_all = joined((col_peak, col_mass), "blk", combine_stats)
    col_lse_all = peak_all + jnp.log(mass_all)
    weights = (
        0.5 * (jnp.exp(logits - row_lse[:, None]) + jnp.exp(logits - col_lse_all[None, :]))
    ).astype(jnp.bfloat16)
    grad_image = logit_scale * (
        jnp.dot(weights, all_texts, preferred_element_type=jnp.float32)
        - hat_text.astype(jnp.float32)
    )
    columns = lax.all_to_all(weights, "blk", split_axis=1, concat_axis=0, tiled=True)
    all_images = lax.all_gather(hat_image, "blk", axis=0, tiled=True)
    text_total = contract_first(columns, all_images)
    grad_text = logit_scale * (text_total - hat_image.astype(jnp.float32))
    image_grad = project_back(grad_image, unit_image, inv_image).astype(jnp.bfloat16)
    text_grad = project_back(grad_text, unit_text, inv_text).astype(jnp.bfloat16)
    return (image_grad[None], text_grad[None], d_input[None], kernel_grad, channel_grads)


def solution(mesh):
    placed = (
        P("grp", "blk", None),
        P("grp", "blk", None),
        P(),
        P(("blk", "grp"), None, None, None),
        P(),
        P(),
        P(),
        P(("blk", "grp"), None, None, None),
    )
    return jax.shard_map(
        per_device,
        mesh=mesh,
        in_specs=placed,
        out_specs=(
            P("grp", "blk", None),
            P("grp", "blk", None),
            P(("blk", "grp"), None, None, None),
            P(),
            P(),
        ),
        check_vma=False,
    )
```

profile of v0, /device:TPU:8, one launch (start us, length us, event | category | flops | bytes accessed | tf_op | source)
XLA Modules:
  0.0 696.1 jit_solution(9845682227838339220)
XLA Ops:
  9.1 1.8 fusion.110
  13.9 200.7 %all-gather.7.cloned.1.call-done = bf16[8192,1024]{1,0:T(8,128)(2,1)} async-done(((bf16[128,1024]{1,0:T(8,128)(2,1)}), bf16[8192,1024]{1,0:T(8,128)(2,1)}) %all-gather.7.cloned.1.call-update) | async-done | bytes 16777232 | tf_op jit(solution)/shard_map/all_gather | solution.py:121
  214.5 14.1 %fusion.128 = (f32[128]{0:T(128)S(1)}, f32[8192]{0:T(1024)}, f32[128,8192]{1,0:T(8,128)}) fusion(f32[]{:T(128)S(6)} %copy.28, bf16[128,1024]{1,0:T(8,128)(2,1)S(1)} %fusion.113, bf16[8192,1024]{1,0:T(8,128)(2,1)} %all-gather.7.cloned.1.call-done), kind=kOutput, calls=%fused_computation.302 | convolution fusion | flops 2150621184 | bytes 21266948 | tf_op jit(solution)/shard_map/dot_general | solution.py:38
  229.5 4.1 exponential_reduce_fusion.1
  234.3 4.8 fusion.131
  239.9 2.3 multiply_reduce_fusion
  242.2 1.6 fusion.129
  243.7 2.4 multiply_reduce_fusion.18
  246.2 5.4 concatenate.3
  252.2 91.5 %all-gather.11.cloned.1.call-done = f32[524288]{0:T(1024)} async-done(((f32[8192]{0:T(1024)}), f32[524288]{0:T(1024)}) %all-gather.11.cloned.1.call-update) | async-done | bytes 2097168 | tf_op jit(solution)/shard_map/all_gather | solution.py:14
  343.6 1.6 slice-done
  345.2 1.7 reshape.78
  346.9 115.5 %all-gather.13.cloned.1.call-done = f32[524288]{0:T(1024)} async-done(((f32[8192]{0:T(1024)}), f32[524288]{0:T(1024)}) %all-gather.13.cloned.1.call-update) | async-done | bytes 2097168 | tf_op jit(solution)/shard_map/all_gather | solution.py:14
  462.4 1.6 slice-done.2
  464.0 1.7 reshape.79
  465.7 72.1 %while.12 = (s32[]{:T(128)}, f32[8192]{0:T(1024)S(1)}, f32[8192]{0:T(1024)S(1)}, f32[63,8192]{1,0:T(8,128)}, f32[63,8192]{1,0:T(8,128)}, /*index=5*/s32[]{:T(128)}) while((s32[]{:T(128)}, f32[8192]{0:T(1024)S(1)}, f32[8192]{0:T(1024)S(1)}, f32[63,8192]{1,0:T(8,128)}, f32[63,8192]{1,0:T(8,128)}, /*index=5*/s32[]{:T(128)}) %tuple.156), condition=%wide.region_7.8_spmd, body=%wide.region_6.7_spmd.sunk | while | flops 49154 | bytes 327761 | solution.py:17
  476.0 1.1 constant_dynamic-slice_fusion.3
  477.1 1.1 constant_dynamic-slice_fusion.3
  490.8 1.1 constant_dynamic-slice_fusion.3
  514.8 1.2 constant_dynamic-slice_fusion.3
  522.9 1.1 constant_dynamic-slice_fusion.3
  526.3 1.1 constant_dynamic-slice_fusion.3
  532.0 1.1 constant_dynamic-slice_fusion.3
  533.2 1.1 constant_dynamic-slice_fusion.3
  535.5 1.1 constant_dynamic-slice_fusion.3
  537.8 4.8 copy_bitcast_fusion
  542.6 8.8 %all-to-all-start = ((bf16[128,64,128]{2,0,1:T(8,128)(2,1)}), bf16[128,64,128]{2,0,1:T(8,128)(2,1)S(1)}, u32[]{:S(2)}, u32[]{:S(2)}) async-start(bf16[128,64,128]{2,0,1:T(8,128)(2,1)} %copy_bitcast_fusion), calls=%async_computation | async-start | bytes 4194304 | tf_op jit(solution)/shard_map/all_to_all | solution.py:135
  551.4 5.6 fusion.124
  557.1 1.3 broadcast_multiply_fusion
  560.0 10.0 %fusion.114 = (f32[128]{0:T(128)S(1)}, f32[128,1024]{1,0:T(8,128)S(1)}) fusion(bf16[1,128,1024]{2,1,0:T(8,128)(2,1)S(1)} %copy-done.4, f32[128]{0:T(128)S(1)} %copy-done.43, bf16[128,1024]{1,0:T(8,128)(2,1)S(1)} %copy-done.7, bf16[8192,1024]{1,0:T(8,128)(2,1)} %all-gather.7.cloned.1.call-done, f32[128,8192]{1,0:T(8,128)} %get-tuple-element.170, ...), kind=kOutput, calls=%fused_computation.278 | convolution fusion | flops 2153644032 | bytes 22054404 | tf_op jit(solution)/shard_map/dot_general | solution.py:132
  571.0 108.8 %all-gather.9.cloned.1.call-done = bf16[8192,1024]{1,0:T(8,128)(2,1)} async-done(((bf16[128,1024]{1,0:T(8,128)(2,1)}), bf16[8192,1024]{1,0:T(8,128)(2,1)}) %all-gather.9.cloned.1.call-update) | async-done | bytes 16777232 | tf_op jit(solution)/shard_map/all_gather | solution.py:136
  679.8 8.2 %fusion.119 = (f32[128]{0:T(128)S(1)}, f32[128,1024]{1,0:T(8,128)S(1)}) fusion(bf16[1,128,1024]{2,1,0:T(8,128)(2,1)S(1)} %copy-done.2, f32[128]{0:T(128)S(1)} %add_rsqrt_fusion.1, bf16[128,1024]{1,0:T(8,128)(2,1)S(1)} %copy-done.1, bf16[8192,128]{1,0:T(8,128)(2,1)S(1)} %bitcast.165, bf16[8192,1024]{1,0:T(8,128)(2,1)} %all-gather.9.cloned.1.call-done, ...), kind=kOutput, calls=%fused_computation.283 | convolution fusion | flops 2148401152 | bytes 19923972 | tf_op jit(solution)/shard_map/dot_general | solution.py:44
  (250 shorter events, 70.1 us)
Async XLA Ops:
  8.0 206.5 %all-gather.7.cloned.1.call-start = ((), (), s32[]{:S(2)}) async-start(), calls=%async_computation.1 | async-start | bytes 17039360 | tf_op jit(solution)/shard_map/all_gather | solution.py:121
  10.9 332.7 %all-gather.11.cloned.1.call-start = ((), (), s32[]{:S(2)}) async-start(), calls=%async_computation.4 | async-start | bytes 2129920 | tf_op jit(solution)/shard_map/all_gather | solution.py:14
  12.7 215.9 %copy-start.42 = (f32[128]{0:T(128)}, f32[128]{0:T(128)S(1)}, u32[]{:S(2)}) copy-start(f32[128]{0:T(128)S(1)} %add_rsqrt_fusion.2) | copy-start | bytes 1540
  13.8 214.8 %copy-start = (bf16[128,1024]{1,0:T(8,128)(2,1)}, bf16[128,1024]{1,0:T(8,128)(2,1)S(1)}, u32[]{:S(2)}) copy-start(bf16[128,1024]{1,0:T(8,128)(2,1)S(1)} %fusion.113) | copy-start | bytes 786436
  13.8 214.9 %copy-start.40 = (bf16[3072]{0:T(1024)(128)(2,1)S(1)}, bf16[3072]{0:T(1024)(128)(2,1)}, u32[]{:S(2)}) copy-start(bf16[3072]{0:T(1024)(128)(2,1)} %param.15) | copy-start | bytes 18436
  13.8 214.9 %copy-start.41 = (bf16[3072]{0:T(1024)(128)(2,1)S(1)}, bf16[3072]{0:T(1024)(128)(2,1)}, u32[]{:S(2)}) copy-start(bf16[3072]{0:T(1024)(128)(2,1)} %param.16) | copy-start | bytes 18436
  13.8 214.9 %copy-start.3 = (bf16[1,7,7,3072]{3,2,1,0:T(8,128)(2,1)S(1)}, bf16[1,7,7,3072]{3,2,1,0:T(8,128)(2,1)}, u32[]{:S(2)}) copy-start(bf16[1,7,7,3072]{3,2,1,0:T(8,128)(2,1)} %param.17) | copy-start | bytes 903172
  13.8 215.0 %copy-start.6 = (bf16[7,7,3072]{2,1,0:T(8,128)(2,1)S(1)}, bf16[7,7,3072]{2,1,0:T(8,128)(2,1)}, u32[]{:S(2)}) copy-start(bf16[7,7,3072]{2,1,0:T(8,128)(2,1)} %param.14) | copy-start | bytes 903172
  228.6 233.8 %all-gather.13.cloned.1.call-start = ((), (), s32[]{:S(2)}) async-start(), calls=%async_computation.5 | async-start | bytes 2129920 | tf_op jit(solution)/shard_map/all_gather | solution.py:14
  229.0 5.0 copy-start.8
  229.0 5.0 copy-start.9
  229.0 5.0 copy-start.10
  229.0 5.0 copy-start.11
  229.0 5.0 copy-start.12
  229.0 5.0 copy-start.13
  229.1 5.0 copy-start.14
  229.1 5.0 copy-start.15
  229.1 5.0 copy-start.16
  229.1 5.0 copy-start.17
  229.1 5.0 copy-start.18
  229.1 5.0 copy-start.19
  229.1 5.0 copy-start.20
  229.3 4.8 copy-start.21
  229.3 4.8 copy-start.22
  233.6 323.5 %all-reduce.4.cloned.1.call-start = ((), (), s32[]{:S(2)}) async-start(), calls=%async_computation.3 | async-start | bytes 1376256 | tf_op jit(solution)/shard_map/psum | solution.py:113
  251.6 428.2 %all-gather.9.cloned.1.call-start = ((), (), s32[]{:S(2)}) async-start(), calls=%async_computation.2 | async-start | bytes 17039360 | tf_op jit(solution)/shard_map/all_gather | solution.py:136
  252.2 285.7 %copy-start.44 = (f32[128]{0:T(128)}, f32[128]{0:T(128)S(1)}, u32[]{:S(2)}) copy-start(f32[128]{0:T(128)S(1)} %log_add_fusion.1) | copy-start | bytes 1540
  542.6 137.2 %all-to-all-start = ((bf16[128,64,128]{2,0,1:T(8,128)(2,1)}), bf16[128,64,128]{2,0,1:T(8,128)(2,1)S(1)}, u32[]{:S(2)}, u32[]{:S(2)}) async-start(bf16[128,64,128]{2,0,1:T(8,128)(2,1)} %copy_bitcast_fusion), calls=%async_computation | async-start | bytes 4194304 | tf_op jit(solution)/shard_map/all_to_all | solution.py:135
  551.4 8.6 %copy-start.4 = (bf16[1,128,1024]{2,1,0:T(8,128)(2,1)S(1)}, bf16[1,128,1024]{2,1,0:T(8,128)(2,1)}, u32[]{:S(2)}) copy-start(bf16[1,128,1024]{2,1,0:T(8,128)(2,1)} %param.10) | copy-start | bytes 786436
  551.4 8.6 %copy-start.7 = (bf16[128,1024]{1,0:T(8,128)(2,1)S(1)}, bf16[128,1024]{1,0:T(8,128)(2,1)}, u32[]{:S(2)}) copy-start(bf16[128,1024]{1,0:T(8,128)(2,1)} %fusion.110) | copy-start | bytes 786436
  560.0 119.8 %copy-start.1 = (bf16[128,1024]{1,0:T(8,128)(2,1)S(1)}, bf16[128,1024]{1,0:T(8,128)(2,1)}, u32[]{:S(2)}) copy-start(bf16[128,1024]{1,0:T(8,128)(2,1)} %copy-done) | copy-start | bytes 786436
  560.0 119.8 %copy-start.2 = (bf16[1,128,1024]{2,1,0:T(8,128)(2,1)S(1)}, bf16[1,128,1024]{2,1,0:T(8,128)(2,1)}, u32[]{:S(2)}) copy-start(bf16[1,128,1024]{2,1,0:T(8,128)(2,1)} %param.11) | copy-start | bytes 786436
  (24 other events, 99.5 us)
Sparse Core Ops, SparseCore 0:
  13.0 201.4 all-gather.6
  228.7 114.8 all-gather.10
  347.8 114.5 all-gather.12
  465.9 213.8 all-gather.8
Sparse Core Ops, SparseCore 1:
  251.6 256.2 all-reduce.3
where the time goes:
time: 699 us; the launch traced here: 696 us
  waiting for transfers between devices  517 us (74%)
  local copies, waits for them, and re-layouts  82.6 us (12%)
  other arithmetic  37.1 us (5%)
  matrix products  32.3 us (5%)
  between operations  16.7 us (2%)
  starting transfers between devices  9.2 us (1%)
    all_gather x2, waiting for transfers between devices, joined(): pieces = jax.tree.map(lambda part: lax.all_gather(part, axis), value)  207 us
    all_gather x1, waiting for transfers between devices, per_device(): all_texts = lax.all_gather(hat_text, 'blk', axis=0, tiled=True)  201 us
    all_gather x1, waiting for transfers between devices, per_device(): all_images = lax.all_gather(hat_image, 'blk', axis=0, tiled=True)  109 us
    dynamic_slice x63, local copies, waits for them, and re-layouts, joined(): lax.scan(lambda subtotal, section: (join(subtotal, section), None), head,...  68.4 us
    dot_general x1, matrix products, contract_last(): lax.dot_general(left_side, right_side, (((1,), (1,)), ((), ())), preferre...  14.1 us
  transfers between devices with their start and end apart: 6, of which 4 were waited for; matrix products, arithmetic and copies ran while one was open for 18% of the time, Pallas kernels for 0%

commit v1 on v0

v1 whole, which is shorter than its diff:
```python
import functools
import jax
import jax.numpy as jnp
from jax import lax
from jax.experimental import pallas as pl
from jax.experimental.pallas import tpu as pltpu
from jax.sharding import PartitionSpec as P

GRID = 7
KS = 7
EPS = 1e-06
LANES = 128
TILES = 24
SPOTS = GRID * GRID
HALF = KS // 2


def spot_mean(value, count):
    folded = value[:, 0:8] + value[:, 8:16] + value[:, 16:24]
    folded = jnp.sum(folded, axis=1, keepdims=True)
    return jnp.sum(folded, axis=2, keepdims=True) * (1.0 / count)


def conv_kernel(x_ref, g_ref, k_ref, bias_ref, gain_ref, din_ref, kg_ref, cg_ref, xs, gs, ks, cs, ds, bs, acc):
    channels = TILES * LANES

    def spread(src, dst):
        for y in range(GRID):
            for t in range(TILES):
                dst[pl.ds(y * GRID * TILES + t, GRID, stride=TILES), :] = src[
                    y, :, t * LANES : (t + 1) * LANES
                ].astype(jnp.float32)

    spread(x_ref, xs)
    spread(k_ref, ks)
    spread(g_ref, gs)
    for t in range(TILES):
        bs[t : t + 1, :] = bias_ref[0:1, t * LANES : (t + 1) * LANES].astype(jnp.float32)
        bs[TILES + t : TILES + t + 1, :] = gain_ref[0:1, t * LANES : (t + 1) * LANES].astype(jnp.float32)

    def rows(part, spot):
        return pl.ds(pl.multiple_of(spot * TILES + part * 8, 8), 8)

    def gather(src, part, row):
        return [src[rows(part, row * GRID + x), :] for x in range(GRID)]

    @pl.loop(0, TILES // 8)
    def _(part):
        bias = bs[pl.ds(pl.multiple_of(part * 8, 8), 8), :]
        for y in range(GRID):
            sums = [bias] * GRID
            for a in range(KS):
                if not 0 <= y + a - HALF < GRID:
                    continue
                left = gather(xs, part, y + a - HALF)
                taps = gather(ks, part, a)
                for x in range(GRID):
                    for b in range(KS):
                        if 0 <= x + b - HALF < GRID:
                            sums[x] = sums[x] + left[x + b - HALF] * taps[b]
            for x in range(GRID):
                cs[rows(part, y * GRID + x), :] = sums[x]

    gain = bs[TILES : 2 * TILES, :][None]
    dsum = jnp.zeros((TILES, LANES), jnp.float32)
    nsum = jnp.zeros((TILES, LANES), jnp.float32)
    gsum = jnp.zeros((TILES, LANES), jnp.float32)
    for y in range(GRID):
        span = slice(y * GRID * TILES, (y + 1) * GRID * TILES)
        conv = cs[span, :].reshape(GRID, TILES, LANES)
        grad = gs[span, :].reshape(GRID, TILES, LANES)
        centre = conv - spot_mean(conv, channels)
        d_normed = grad * gain
        inv = lax.rsqrt(spot_mean(centre * centre, channels) + EPS)
        normed = centre * inv
        d_conv = inv * (
            d_normed - spot_mean(d_normed, channels) - normed * spot_mean(d_normed * normed, channels)
        )
        ds[span, :] = d_conv.reshape(GRID * TILES, LANES)
        dsum = dsum + jnp.sum(d_conv, axis=0)
        nsum = nsum + jnp.sum(grad * normed, axis=0)
        gsum = gsum + jnp.sum(grad, axis=0)
    cg_ref[0] = dsum
    cg_ref[1] = nsum
    cg_ref[2] = gsum

    @pl.loop(0, TILES // 8)
    def _(part):
        for y in range(GRID):
            sums = [None] * GRID
            for a in range(KS):
                if not 0 <= y - a + HALF < GRID:
                    continue
                left = gather(ds, part, y - a + HALF)
                taps = gather(ks, part, a)
                for x in range(GRID):
                    for b in range(KS):
                        if 0 <= x - b + HALF < GRID:
                            term = left[x - b + HALF] * taps[b]
                            sums[x] = term if sums[x] is None else sums[x] + term
            for x in range(GRID):
                cs[rows(part, y * GRID + x), :] = sums[x]
        for a in range(KS):
            sums = [None] * KS
            for y in range(GRID):
                if not 0 <= y + a - HALF < GRID:
                    continue
                left = gather(ds, part, y)
                right = gather(xs, part, y + a - HALF)
                for b in range(KS):
                    for x in range(GRID):
                        if 0 <= x + b - HALF < GRID:
                            term = left[x] * right[x + b - HALF]
                            sums[b] = term if sums[b] is None else sums[b] + term
            for b in range(KS):
                kg_ref[a * KS + b, pl.ds(pl.multiple_of(part * 8, 8), 8), :] = sums[b]

    for y in range(GRID):
        for t in range(TILES):
            din_ref[y, :, t * LANES : (t + 1) * LANES] = cs[
                pl.ds(y * GRID * TILES + t, GRID, stride=TILES), :
            ].astype(jnp.bfloat16)


def conv_block(x, g, k, bias, gain):
    f32 = jnp.float32
    big = pltpu.VMEM((SPOTS * TILES, LANES), f32)
    return pl.pallas_call(
        conv_kernel,
        out_shape=(
            jax.ShapeDtypeStruct((GRID, GRID, TILES * LANES), jnp.bfloat16),
            jax.ShapeDtypeStruct((SPOTS, TILES, LANES), f32),
            jax.ShapeDtypeStruct((3, TILES, LANES), f32),
        ),
        in_specs=[pl.BlockSpec(memory_space=pltpu.VMEM)] * 5,
        out_specs=[pl.BlockSpec(memory_space=pltpu.VMEM)] * 3,
        scratch_shapes=[big, big, big, big, big, pltpu.VMEM((2 * TILES, LANES), f32), pltpu.VMEM((8, LANES), f32)],
        compiler_params=pltpu.CompilerParams(vmem_limit_bytes=24 << 20),
        cost_estimate=pl.CostEstimate(flops=30_000_000, bytes_accessed=2_500_000, transcendentals=49),
    )(x, g, k, bias.reshape(1, -1), gain.reshape(1, -1))


AROUND = 8


def normalize(raw):
    values = raw.astype(jnp.float32)
    inverse = lax.rsqrt(jnp.sum(values * values, axis=-1, keepdims=True) + EPS)
    return (values * inverse, inverse)


def project_back(grad_hat, unit_hat, inverse):
    along = jnp.sum(grad_hat * unit_hat, axis=-1, keepdims=True)
    return inverse * (grad_hat - along * unit_hat)


def contract(left, right, dims):
    return lax.dot_general(left, right, ((dims[0], dims[1]), ((), ())), preferred_element_type=jnp.float32)


def lse_over(logits, axis, groups):
    peak = jnp.max(logits, axis=axis)
    mass = jnp.sum(jnp.exp(logits - jnp.expand_dims(peak, axis)), axis=axis)
    both = lax.all_gather(jnp.stack([peak, mass]), "blk", axis_index_groups=groups)
    top = jnp.max(both[:, 0], axis=0)
    return top + jnp.log(jnp.sum(both[:, 1] * jnp.exp(both[:, 0] - top), axis=0))


def per_device(
    image_embed, text_embed, logit_scale, block_input, dw_kernel, dw_bias, ln_gain, block_grad
):
    d_input, kterm, cterm = conv_block(block_input[0], block_grad[0], dw_kernel, dw_bias, ln_gain)
    totals = lax.psum(jnp.concatenate([kterm, cterm], axis=0), ("blk", "grp"))
    totals = totals / (lax.axis_size("blk") * lax.axis_size("grp"))
    kernel_grad = totals[:SPOTS].reshape(KS, KS, TILES * LANES)
    channel_grads = totals[SPOTS:].reshape(3, TILES * LANES)
    lines = [[z * AROUND + b for z in range(AROUND)] for b in range(AROUND)]
    sheets = [[z * AROUND + b for b in range(AROUND)] for z in range(AROUND)]
    unit_image, inv_image = normalize(image_embed[0])
    unit_text, inv_text = normalize(text_embed[0])
    hat_image = unit_image.astype(jnp.bfloat16)
    hat_text = unit_text.astype(jnp.bfloat16)
    images = lax.all_gather(hat_image, "blk", axis=0, tiled=True, axis_index_groups=sheets)
    texts = lax.all_gather(hat_text, "blk", axis=0, tiled=True, axis_index_groups=lines)
    logits = contract(images, texts, ((1,), (1,))) * logit_scale
    row_lse = lse_over(logits, 1, sheets)
    col_lse = lse_over(logits, 0, lines)
    weights = (
        0.5 * (jnp.exp(logits - row_lse[:, None]) + jnp.exp(logits - col_lse[None, :]))
    ).astype(jnp.bfloat16)
    part_image = contract(weights, texts, ((1,), (0,))).astype(jnp.bfloat16)
    part_text = contract(weights, images, ((0,), (0,))).astype(jnp.bfloat16)
    sum_image = lax.psum_scatter(part_image, "blk", axis_index_groups=sheets, tiled=True)
    sum_text = lax.psum_scatter(part_text, "blk", axis_index_groups=lines, tiled=True)
    grad_image = logit_scale * (sum_image.astype(jnp.float32) - hat_text.astype(jnp.float32))
    grad_text = logit_scale * (sum_text.astype(jnp.float32) - hat_image.astype(jnp.float32))
    image_grad = project_back(grad_image, unit_image, inv_image).astype(jnp.bfloat16)
    text_grad = project_back(grad_text, unit_text, inv_text).astype(jnp.bfloat16)
    return (image_grad[None], text_grad[None], d_input[None], kernel_grad, channel_grads)


def solution(mesh):
    placed = (
        P("grp", "blk", None),
        P("grp", "blk", None),
        P(),
        P(("blk", "grp"), None, None, None),
        P(),
        P(),
        P(),
        P(("blk", "grp"), None, None, None),
    )
    return jax.shard_map(
        per_device,
        mesh=mesh,
        in_specs=placed,
        out_specs=(
            P("grp", "blk", None),
            P("grp", "blk", None),
            P(("blk", "grp"), None, None, None),
            P(),
            P(),
        ),
        check_vma=False,
    )
```

time: 699 us -> 322 us (0.46)
  waiting for transfers between devices: 517 us -> 202 us
  local copies, waits for them, and re-layouts: 82.6 us -> 5.96 us
  blocking collectives: 0 us -> 58.9 us
  other arithmetic: 37.1 us -> 16.1 us
  matrix products: 32.3 us -> 16.1 us
  starting transfers between devices: 9.2 us -> 0.39 us
    all_gather x4 -> x2, waiting for transfers between devices: 516 us -> 92.4 us  [the longest x1 49 us: per_device(): lax.all_gather(hat_image, 'blk', axis=0, tiled=True, axis_index_groups=sh...]
    psum x1, waiting for transfers between devices: 0.03 us -> 97.2 us  [per_device(): totals = lax.psum(jnp.concatenate([kterm, cterm], axis=0), ('blk', 'grp'))]
    dynamic_slice x63 -> x0, local copies, waits for them, and re-layouts: 68.4 us -> none  [joined(): lax.scan(lambda subtotal, section: (join(subtotal, section), None), head,...]
    all_gather x0 -> x2, blocking collectives: none -> 58.9 us  [lse_over(): lax.all_gather(jnp.stack([peak, mass]), 'blk', axis_index_groups=groups)]
    dot_general x3, matrix products: 32.3 us -> 16.1 us  [contract(): lax.dot_general(left, right, ((dims[0], dims[1]), ((), ())), preferred_el...]
    reduce_scatter x0 -> x2, waiting for transfers between devices: none -> 12.5 us  [the longest x1 12.5 us: per_device(): lax.psum_scatter(part_image, 'blk', axis_index_groups=sheets, tiled=True)]
    reduce_sum x8 -> x6, other arithmetic: 16 us -> 4.34 us  [the longest x2 2.52 us: project_back(): along = jnp.sum(grad_hat * unit_hat, axis=-1, keepdims=True)]
    all_to_all x1 -> x0, starting transfers between devices: 8.81 us -> none  [per_device(): lax.all_to_all(weights, 'blk', split_axis=1, concat_axis=0, tiled=True)]
  transfers between devices with their start and end apart: 6 -> 5, of which waited for: 4 -> 4; matrix products, arithmetic and copies ran while one was open for 18% -> 9% of each run, Pallas kernels for 0% -> 2%
where the time goes in v1:
time: 322 us; the launch traced here: 321 us
  waiting for transfers between devices  202 us (63%)
  blocking collectives  58.9 us (18%)
  other arithmetic  16.1 us (5%)
  matrix products  16.1 us (5%)
  between operations  16 us (5%)
  local copies, waits for them, and re-layouts  5.96 us (2%)
  Pallas kernels  5.47 us (2%)
    psum x1, waiting for transfers between devices, per_device(): totals = lax.psum(jnp.concatenate([kterm, cterm], axis=0), ('blk', 'grp'))  97.2 us
    all_gather x2, blocking collectives, lse_over(): lax.all_gather(jnp.stack([peak, mass]), 'blk', axis_index_groups=groups)  58.9 us
    all_gather x1, waiting for transfers between devices, per_device(): lax.all_gather(hat_image, 'blk', axis=0, tiled=True, axis_index_groups=sh...  49 us
    all_gather x1, waiting for transfers between devices, per_device(): lax.all_gather(hat_text, 'blk', axis=0, tiled=True, axis_index_groups=lines)  43.4 us
    dot_general x3, matrix products, contract(): lax.dot_general(left, right, ((dims[0], dims[1]), ((), ())), preferred_el...  16.1 us
    reduce_scatter x1, waiting for transfers between devices, per_device(): lax.psum_scatter(part_image, 'blk', axis_index_groups=sheets, tiled=True)  12.5 us
  transfers between devices with their start and end apart: 5, of which 4 were waited for; matrix products, arithmetic and copies ran while one was open for 9% of the time, Pallas kernels for 2%

profile of v1, /device:TPU:8, one launch (start us, length us, event | category | flops | bytes accessed | tf_op | source)
XLA Modules:
  0.0 320.9 jit_solution(6076750854063039750)
XLA Ops:
  8.0 1.1 fusion.10
  9.1 1.8 fusion.5
  11.0 1.1 fusion.15
  12.1 1.8 fusion.2
  13.9 0.0 all-reduce.2.cloned.1.call-start
  13.9 0.7 reshape.56.bias_ref
  14.6 0.7 reshape.57.gain_ref
  15.3 1.0 copy-done
  16.3 1.0 copy-done.1
  17.3 1.0 copy-done.2
  18.3 5.5 %shard_map.119 = (bf16[7,7,3072]{2,1,0:T(8,128)(2,1)}, f32[49,24,128]{2,1,0:T(8,128)S(1)}, f32[3,24,128]{2,1,0:T(8,128)S(1)}) custom-call(bf16[7,7,3072]{2,1,0:T(8,128)(2,1)S(1)} %bitcast.68, bf16[7,7,3072]{2,1,0:T(8,128)(2,1)S(1)} %bitcast.69, bf16[7,7,3072]{2,1,0:T(8,128)(2,1)S(1)} %copy-done.2, bf16[1,3072]{1,0:T(2,128)(2,1)S(1)} %reshape.56.bias_ref, ...), custom_call_target="tpu_custom_call" | custom-call | flops 30000000 | bytes 2500000 | tf_op jit(solution)/shard_map/pallas_call | solution.py:128
  23.7 0.9 pad_maximum_fusion
  25.3 49.0 %all-gather.7.cloned.1.call-done = bf16[1024,1024]{1,0:T(8,128)(2,1)} async-done(((bf16[128,1024]{1,0:T(8,128)(2,1)}), bf16[1024,1024]{1,0:T(8,128)(2,1)}) %all-gather.7.cloned.1.call-update) | async-done | bytes 2097168 | tf_op jit(solution)/shard_map/all_gather | solution.py:183
  74.3 43.4 %all-gather.9.cloned.1.call-done = bf16[1024,1024]{1,0:T(8,128)(2,1)} async-done(((bf16[128,1024]{1,0:T(8,128)(2,1)}), bf16[1024,1024]{1,0:T(8,128)(2,1)}) %all-gather.9.cloned.1.call-update) | async-done | bytes 2097168 | tf_op jit(solution)/shard_map/all_gather | solution.py:184
  117.7 4.7 %multiply_reduce_fusion.1 = (f32[1024]{0:T(1024)S(1)}, f32[1024,1024]{1,0:T(8,128)S(1)}) fusion(f32[]{:T(128)S(6)} %copy.37, bf16[1024,1024]{1,0:T(8,128)(2,1)} %all-gather.7.cloned.1.call-done, bf16[1024,1024]{1,0:T(8,128)(2,1)} %all-gather.9.cloned.1.call-done), kind=kOutput, calls=%fused_computation.4 | convolution fusion | flops 2149579776 | bytes 8392708 | tf_op jit(solution)/shard_map/dot_general | solution.py:158
  122.4 1.0 exponential_reduce_fusion.1
  123.5 0.7 exponential_reduce_fusion
  124.2 24.7 %all-gather.3 = f32[8,2,1024]{2,1,0:T(2,128)S(1)} all-gather(f32[1,2,1024]{2,1,0:T(2,128)S(1)} %maximum_bitcast_fusion.1), channel_id=3, replica_groups={{0,32,64,96,128,160,192,224},{4,36,68,100,132,164,196,228},{8,40,72,104..., dimensions={0}, use_global_device_ids=true | all-gather | bytes 73728 | tf_op jit(solution)/shard_map/all_gather | solution.py:164
  148.9 34.2 %all-gather.2 = f32[8,2,1024]{2,1,0:T(2,128)S(1)} all-gather(f32[1,2,1024]{2,1,0:T(2,128)S(1)} %maximum_bitcast_fusion), channel_id=2, replica_groups={{0,4,8,12,16,20,24,28},{32,36,40,44,48,52,56,60},{64,68,72,76,80,84,88,..., dimensions={0}, use_global_device_ids=true | all-gather | bytes 73728 | tf_op jit(solution)/shard_map/all_gather | solution.py:164
  183.1 0.1 fusion.24
  183.3 4.4 %convolution_convert_fusion = bf16[1024,1024]{1,0:T(8,128)(2,1)} fusion(bf16[1024,1024]{1,0:T(8,128)(2,1)S(1)} %copy-done.6, f32[1024,1024]{1,0:T(8,128)S(1)} %get-tuple-element.20, f32[1024]{0:T(1024)S(1)} %log_add_fusion, f32[1024]{0:T(1024)S(1)} %log_add_fusion.1, f32[]{:T(128)S(6)} %copy.37), kind=kOutput, calls=%fused_computation.5 | convolution fusion | flops 2154823680 | bytes 8396804 | tf_op jit(solution)/shard_map/dot_general | solution.py:158
  187.8 0.2 reduce-scatter.3.cloned.1.call-start
  188.0 6.9 %convolution_convert_fusion.1 = bf16[1024,1024]{1,0:T(8,128)(2,1)} fusion(bf16[1024,1024]{1,0:T(8,128)(2,1)} %all-gather.9.cloned.1.call-done, f32[1024,1024]{1,0:T(8,128)} %copy-done.3, f32[1024]{0:T(1024)S(1)} %log_add_fusion, f32[1024]{0:T(1024)S(1)} %log_add_fusion.1, f32[]{:T(128)S(6)} %copy.37), kind=kOutput, calls=%fused_computation.6 | convolution fusion | flops 2154823680 | bytes 8396804 | tf_op jit(solution)/shard_map/dot_general | solution.py:158
  195.0 97.2 %all-reduce.2.cloned.1.call-done = f32[52,24,128]{2,1,0:T(8,128)} async-done(((f32[52,24,128]{2,1,0:T(8,128)}), f32[52,24,128]{2,1,0:T(8,128)}) %all-reduce.2.cloned.1.call-update) | async-done | bytes 638992 | tf_op jit(solution)/shard_map/psum | solution.py:173
  292.2 1.1 broadcast_multiply_fusion
  293.3 0.9 reshape.58
  294.3 0.6 copy.35
  294.9 1.3 fusion.11
  296.2 2.0 fusion.16
  298.2 12.5 %reduce-scatter.3.cloned.1.call-done = bf16[128,1024]{1,0:T(8,128)(2,1)} async-done(((bf16[1024,1024]{1,0:T(8,128)(2,1)}), bf16[128,1024]{1,0:T(8,128)(2,1)}) %reduce-scatter.3.cloned.1.call-update) | async-done | bytes 262160 | tf_op jit(solution)/shard_map/reduce_scatter | solution.py:193
  310.6 1.3 fusion.6
  311.9 2.0 fusion.17
  (30 shorter events, 0.4 us)
Async XLA Ops:
  8.0 66.3 %all-gather.7.cloned.1.call-start = ((), (), s32[]{:S(2)}) async-start(), calls=%async_computation.2 | async-start | bytes 2359296 | tf_op jit(solution)/shard_map/all_gather | solution.py:183
  10.9 106.8 %all-gather.9.cloned.1.call-start = ((), (), s32[]{:S(2)}) async-start(), calls=%async_computation.3 | async-start | bytes 2359296 | tf_op jit(solution)/shard_map/all_gather | solution.py:184
  13.9 278.3 %all-reduce.2.cloned.1.call-start = ((), (), s32[]{:S(2)}) async-start(), calls=%async_computation.6 | async-start | bytes 1277952 | tf_op jit(solution)/shard_map/psum | solution.py:173
  15.3 1.0 copy-start
  16.3 1.0 copy-start.1
  17.3 1.0 copy-start.2
  24.6 270.3 %reduce-scatter.5.cloned.1.call-start = ((), (), s32[]{:S(2)}) async-start(), calls=%async_computation.5 | async-start | bytes 2359296 | tf_op jit(solution)/shard_map/reduce_scatter | solution.py:194
  122.4 60.9 %copy-start.3 = (f32[1024,1024]{1,0:T(8,128)}, f32[1024,1024]{1,0:T(8,128)S(1)}, u32[]{:S(2)}) copy-start(f32[1024,1024]{1,0:T(8,128)S(1)} %get-tuple-element.20) | copy-start | bytes 12582916
  122.4 60.9 %copy-start.6 = (bf16[1024,1024]{1,0:T(8,128)(2,1)S(1)}, bf16[1024,1024]{1,0:T(8,128)(2,1)}, u32[]{:S(2)}) copy-start(bf16[1024,1024]{1,0:T(8,128)(2,1)} %all-gather.7.cloned.1.call-done) | copy-start | bytes 6291460
  187.8 122.8 %reduce-scatter.3.cloned.1.call-start = ((), (), s32[]{:S(2)}) async-start(), calls=%async_computation.4 | async-start | bytes 2359296 | tf_op jit(solution)/shard_map/reduce_scatter | solution.py:193
  195.0 99.9 %copy-start.4 = (bf16[1,128,1024]{2,1,0:T(8,128)(2,1)S(1)}, bf16[1,128,1024]{2,1,0:T(8,128)(2,1)}, u32[]{:S(2)}) copy-start(bf16[1,128,1024]{2,1,0:T(8,128)(2,1)} %param.8) | copy-start | bytes 786436
  195.0 99.9 %copy-start.5 = (bf16[1,128,1024]{2,1,0:T(8,128)(2,1)S(1)}, bf16[1,128,1024]{2,1,0:T(8,128)(2,1)}, u32[]{:S(2)}) copy-start(bf16[1,128,1024]{2,1,0:T(8,128)(2,1)} %param.9) | copy-start | bytes 786436
Sparse Core Ops, SparseCore 0:
  12.0 62.2 all-gather.6
  76.7 41.0 all-gather.8
  187.9 40.2 reduce-scatter.4
  232.2 78.4 reduce-scatter.2
Sparse Core Ops, SparseCore 1:
  24.7 267.4 all-reduce.1

commit v2 on v1

v2 whole, which is shorter than its diff:
```python
import functools
import math

import jax
import jax.numpy as jnp
from jax import lax
from jax.experimental import pallas as pl
from jax.experimental.pallas import tpu as pltpu
from jax.sharding import PartitionSpec as P

GRID = 7
KS = 7
EPS = 1e-06
LANES = 128
TILES = 24
SPOTS = GRID * GRID
HALF = KS // 2


def spot_mean(value, count):
    folded = value[:, 0:8] + value[:, 8:16] + value[:, 16:24]
    folded = jnp.sum(folded, axis=1, keepdims=True)
    return jnp.sum(folded, axis=2, keepdims=True) * (1.0 / count)


def conv_kernel(x_ref, g_ref, k_ref, bias_ref, gain_ref, din_ref, terms_ref, xs, gs, ks, cs, ds, bs):
    channels = TILES * LANES

    def spread(src, dst):
        for y in range(GRID):
            for t in range(TILES):
                dst[pl.ds(y * GRID * TILES + t, GRID, stride=TILES), :] = src[
                    y, :, t * LANES : (t + 1) * LANES
                ].astype(jnp.float32)

    spread(x_ref, xs)
    spread(k_ref, ks)
    spread(g_ref, gs)
    for t in range(TILES):
        bs[t : t + 1, :] = bias_ref[0:1, t * LANES : (t + 1) * LANES].astype(jnp.float32)
        bs[TILES + t : TILES + t + 1, :] = gain_ref[0:1, t * LANES : (t + 1) * LANES].astype(jnp.float32)

    def rows(part, spot):
        return pl.ds(pl.multiple_of(spot * TILES + part * 8, 8), 8)

    def gather(src, part, row):
        return [src[rows(part, row * GRID + x), :] for x in range(GRID)]

    @pl.loop(0, TILES // 8)
    def _(part):
        bias = bs[pl.ds(pl.multiple_of(part * 8, 8), 8), :]
        for y in range(GRID):
            sums = [bias] * GRID
            for a in range(KS):
                if not 0 <= y + a - HALF < GRID:
                    continue
                left = gather(xs, part, y + a - HALF)
                taps = gather(ks, part, a)
                for x in range(GRID):
                    for b in range(KS):
                        if 0 <= x + b - HALF < GRID:
                            sums[x] = sums[x] + left[x + b - HALF] * taps[b]
            for x in range(GRID):
                cs[rows(part, y * GRID + x), :] = sums[x]

    gain = bs[TILES : 2 * TILES, :][None]
    dsum = jnp.zeros((TILES, LANES), jnp.float32)
    nsum = jnp.zeros((TILES, LANES), jnp.float32)
    gsum = jnp.zeros((TILES, LANES), jnp.float32)
    for y in range(GRID):
        span = slice(y * GRID * TILES, (y + 1) * GRID * TILES)
        conv = cs[span, :].reshape(GRID, TILES, LANES)
        grad = gs[span, :].reshape(GRID, TILES, LANES)
        centre = conv - spot_mean(conv, channels)
        d_normed = grad * gain
        inv = lax.rsqrt(spot_mean(centre * centre, channels) + EPS)
        normed = centre * inv
        d_conv = inv * (
            d_normed - spot_mean(d_normed, channels) - normed * spot_mean(d_normed * normed, channels)
        )
        ds[span, :] = d_conv.reshape(GRID * TILES, LANES)
        dsum = dsum + jnp.sum(d_conv, axis=0)
        nsum = nsum + jnp.sum(grad * normed, axis=0)
        gsum = gsum + jnp.sum(grad, axis=0)
    first = SPOTS * TILES
    for index, total in enumerate((dsum, nsum, gsum)):
        terms_ref[first + index * TILES : first + (index + 1) * TILES, :] = total
    first = first + 3 * TILES
    terms_ref[first:SLACK, :] = jnp.zeros((SLACK - first, LANES), jnp.float32)

    @pl.loop(0, TILES // 8)
    def _(part):
        for y in range(GRID):
            sums = [None] * GRID
            for a in range(KS):
                if not 0 <= y - a + HALF < GRID:
                    continue
                left = gather(ds, part, y - a + HALF)
                taps = gather(ks, part, a)
                for x in range(GRID):
                    for b in range(KS):
                        if 0 <= x - b + HALF < GRID:
                            term = left[x - b + HALF] * taps[b]
                            sums[x] = term if sums[x] is None else sums[x] + term
            for x in range(GRID):
                cs[rows(part, y * GRID + x), :] = sums[x]
        for a in range(KS):
            sums = [None] * KS
            for y in range(GRID):
                if not 0 <= y + a - HALF < GRID:
                    continue
                left = gather(ds, part, y)
                right = gather(xs, part, y + a - HALF)
                for b in range(KS):
                    for x in range(GRID):
                        if 0 <= x + b - HALF < GRID:
                            term = left[x] * right[x + b - HALF]
                            sums[b] = term if sums[b] is None else sums[b] + term
            for b in range(KS):
                terms_ref[rows(part, a * KS + b), :] = sums[b]

    for y in range(GRID):
        for t in range(TILES):
            din_ref[y, :, t * LANES : (t + 1) * LANES] = cs[
                pl.ds(y * GRID * TILES + t, GRID, stride=TILES), :
            ].astype(jnp.bfloat16)


def conv_block(x, g, k, bias, gain):
    f32 = jnp.float32
    big = pltpu.VMEM((SPOTS * TILES, LANES), f32)
    return pl.pallas_call(
        conv_kernel,
        out_shape=(
            jax.ShapeDtypeStruct((GRID, GRID, TILES * LANES), jnp.bfloat16),
            jax.ShapeDtypeStruct((SLACK, LANES), f32),
        ),
        in_specs=[pl.BlockSpec(memory_space=pltpu.VMEM)] * 5,
        out_specs=[pl.BlockSpec(memory_space=pltpu.VMEM)] * 2,
        scratch_shapes=[big, big, big, big, big, pltpu.VMEM((2 * TILES, LANES), f32)],
        compiler_params=pltpu.CompilerParams(vmem_limit_bytes=24 << 20),
        cost_estimate=pl.CostEstimate(flops=30_000_000, bytes_accessed=2_500_000, transcendentals=49),
    )(x, g, k, bias.reshape(1, -1), gain.reshape(1, -1))


ROWS = 128
PART = 64
WIDE = 256
MESH = pl.DeviceIdType.MESH
SLACK = 1280
HIGH_SHIFT = 12.0
LOW_SHIFT = 10.0
LOW_CAP = 30.0
LOW_LIMIT = 55.0


class Geometry:
    def __init__(self, z, y_hi, x, y_lo, core, width):
        self.z, self.y_hi, self.x, self.y_lo, self.core, self.width = z, y_hi, x, y_lo, core, width
        self.sheet = y_hi * x
        self.y = y_hi * y_lo
        self.half = SLACK // core
        self.y_rows = self.half // self.y
        self.x_rows = self.y_rows // x


def dot(left, right, dims=((1,), (0,))):
    return lax.dot_general(left, right, (dims, ((), ())), preferred_element_type=jnp.float32)


def loss_kernel(
    geo, scale_ref, img_ref, txt_ref, terms_ref, ig_ref, tg_ref, kg_ref, cg_ref,
    ia, ta, ui, ut, vi, vt, probs, weights, flip, row_hi, row_lo, alpha, beta, row_all, col_all, gz, gx,
    zout, zin, xout, xin, yout, yin, l1, hsum, l2, qsum, l3, l4, fin,
    zag_s, zag_r, xag_s, xag_r, yag_s, yag_r, row_s, row_r, col_s, col_r,
    zrs_s, zrs_r, xrs_s, xrs_r, yrs_s, yrs_r,
    s1, r1, s2, r2, s3, r3, s4, r4, s5, r5, s6, r6, s7, r7,
):
    f32, bf16 = jnp.float32, jnp.bfloat16
    nz, nx, sheet = geo.z, geo.x, geo.sheet
    blk, grp = lax.axis_index("blk"), lax.axis_index("grp")
    z, b = blk // sheet, lax.rem(blk, sheet)
    yh, x = b // nx, lax.rem(b, nx)
    yl, core = grp // geo.core, lax.rem(grp, geo.core)
    y = yh * geo.y_lo + yl
    hy = 1 - yh

    def place(z_to, yh_to, x_to):
        return {"blk": z_to * sheet + yh_to * nx + x_to, "grp": grp}

    def column(y_to):
        return {
            "blk": z * sheet + (y_to // geo.y_lo) * nx + x,
            "grp": lax.rem(y_to, geo.y_lo) * geo.core + core,
        }

    def turn(value, by, size):
        return lax.rem(value + by + size, size)

    mate = {"blk": blk, "grp": yl * geo.core + (geo.core - 1 - core)}
    facing = place(z, hy, x)
    sent = []

    def copy(src, dst, send, recv, to):
        return pltpu.make_async_remote_copy(
            src_ref=src, dst_ref=dst, send_sem=send, recv_sem=recv, device_id=to, device_id_type=MESH
        )

    def start(*args):
        moving = copy(*args)
        moving.start()
        sent.append(moving)

    def arrived(dst, send, recv):
        copy(dst, dst, send, recv, facing).wait_recv()

    barrier = pltpu.get_barrier_semaphore()
    peers = [place(turn(z, o, nz), yh, x) for o in range(1, nz)]
    for q in range(2):
        for o in range(nx):
            if q or o:
                peers.append(place(z, hy if q else yh, turn(x, o, nx)))
    for o in range(1, geo.y):
        if o != geo.y_lo:
            peers.append(column(turn(y, o, geo.y)))
    peers.append(mate)
    for peer in peers:
        pl.semaphore_signal(barrier, inc=1, device_id=peer, device_id_type=MESH)

    def slot(index, part):
        return pl.ds(pl.multiple_of(index * ROWS + part * PART, PART), PART)

    def full(index):
        return pl.ds(pl.multiple_of(index * ROWS, ROWS), ROWS)

    def unit_rows(raw, unit, inverse, everyone, index):
        values = raw[...].astype(f32)
        inv = lax.rsqrt(jnp.sum(values * values, axis=-1, keepdims=True) + EPS)
        scaled = values * inv
        unit[...] = scaled
        inverse[...] = inv
        everyone[full(index), :] = scaled.astype(bf16)

    unit_rows(txt_ref, ut, vt, ta, z)
    unit_rows(img_ref, ui, vi, ia, b)
    pl.semaphore_wait(barrier, len(peers))

    def sign(d):
        return 1 - 2 * d

    def z_gather(d, k):
        rows = slot(turn(z, -sign(d) * (k // 2), nz), (k % 2) ^ d)
        to = place(turn(z, sign(d), nz), yh, x)
        start(ta.at[rows], ta.at[rows], zag_s.at[d, k], zag_r.at[d, k], to)

    def z_gathered(d, k):
        rows = slot(turn(z, -sign(d) * (k // 2 + 1), nz), (k % 2) ^ d)
        arrived(ta.at[rows], zag_s.at[d, k], zag_r.at[d, k])

    def x_gather(q, d, k):
        rows = slot((hy if q else yh) * nx + turn(x, -sign(d) * (k // 2), nx), (k % 2) ^ d)
        to = place(z, yh, turn(x, sign(d), nx))
        start(ia.at[rows], ia.at[rows], xag_s.at[q, d, k], xag_r.at[q, d, k], to)

    def x_gathered(q, d, k):
        rows = slot((hy if q else yh) * nx + turn(x, -sign(d) * (k // 2 + 1), nx), (k % 2) ^ d)
        arrived(ia.at[rows], xag_s.at[q, d, k], xag_r.at[q, d, k])

    def y_gather(c):
        start(ia.at[slot(b, c)], ia.at[slot(b, c)], yag_s.at[c], yag_r.at[c], facing)

    def y_gathered(c):
        arrived(ia.at[slot(hy * nx + x, c)], yag_s.at[c], yag_r.at[c])

    def share(first, rows):
        return pl.ds(pl.multiple_of(first, 8), rows)

    def mate_send():
        start(terms_ref.at[share((geo.core - 1 - core) * geo.half, geo.half)], l1, s1.at[0], r1.at[0], mate)

    def mate_sum():
        arrived(l1, s1.at[0], r1.at[0])
        hsum[...] = terms_ref[share(core * geo.half, geo.half), :] + l1[...]

    def y_send():
        for o in range(1, geo.y):
            to = turn(y, o, geo.y)
            start(hsum.at[share(to * geo.y_rows, geo.y_rows)], l2.at[o], s2.at[o], r2.at[o], column(to))

    def y_sum():
        total = hsum[share(y * geo.y_rows, geo.y_rows), :]
        for o in range(1, geo.y):
            arrived(l2.at[o], s2.at[o], r2.at[o])
            total = total + l2[o]
        qsum[...] = total

    def x_send():
        for o in range(1, nx):
            to = turn(x, o, nx)
            start(qsum.at[share(to * geo.x_rows, geo.x_rows)], l3.at[o], s3.at[o], r3.at[o], place(z, yh, to))

    def x_sum():
        total = qsum[share(x * geo.x_rows, geo.x_rows), :]
        for o in range(1, nx):
            arrived(l3.at[o], s3.at[o], r3.at[o])
            total = total + l3[o]
        l4[z] = total

    def z_send():
        for o in range(1, nz):
            start(l4.at[z], l4.at[z], s4.at[o], r4.at[o], place(turn(z, o, nz), yh, x))

    mine = core * geo.half + y * geo.y_rows + x * geo.x_rows

    def z_sum():
        for o in range(1, nz):
            arrived(l4.at[turn(z, -o, nz)], s4.at[o], r4.at[o])
        total = l4[0]
        for o in range(1, nz):
            total = total + l4[o]
        fin[share(mine, geo.x_rows), :] = total * (1.0 / (geo.z * geo.sheet * geo.y_lo * geo.core))

    def x_spread():
        rows = fin.at[share(mine, geo.x_rows)]
        for o in range(1, nx):
            start(rows, rows, s5.at[o], r5.at[o], place(z, yh, turn(x, o, nx)))

    def x_spread_done():
        for o in range(1, nx):
            first = core * geo.half + y * geo.y_rows + turn(x, -o, nx) * geo.x_rows
            arrived(fin.at[share(first, geo.x_rows)], s5.at[o], r5.at[o])

    def y_spread():
        rows = fin.at[share(core * geo.half + y * geo.y_rows, geo.y_rows)]
        for o in range(1, geo.y):
            start(rows, rows, s6.at[o], r6.at[o], column(turn(y, o, geo.y)))

    def y_spread_done():
        for o in range(1, geo.y):
            first = core * geo.half + turn(y, -o, geo.y) * geo.y_rows
            arrived(fin.at[share(first, geo.y_rows)], s6.at[o], r6.at[o])

    def mate_spread():
        rows = fin.at[share(core * geo.half, geo.half)]
        start(rows, rows, s7.at[0], r7.at[0], mate)

    def mate_spread_done():
        arrived(fin.at[share((geo.core - 1 - core) * geo.half, geo.half)], s7.at[0], r7.at[0])

    half_scale = scale_ref[0] * 0.5
    row_hi[...] = jnp.zeros_like(row_hi)
    row_lo[...] = jnp.zeros_like(row_lo)
    blocks = nz * ROWS // WIDE
    late = turn(z, nz // 2, nz) // (WIDE // ROWS)

    def logits_block(n):
        lanes = pl.ds(pl.multiple_of(n * WIDE, WIDE), WIDE)

        def rows_step(m, sums):
            rows = pl.ds(pl.multiple_of(m * WIDE, WIDE), WIDE)
            logits = dot(ia[rows, :], ta[lanes, :], ((1,), (1,)))
            root = jnp.exp(logits * half_scale)
            probs[rows, lanes] = root
            high = root * math.exp(-HIGH_SHIFT)
            high = high * high
            low = jnp.minimum(root * math.exp(LOW_SHIFT), math.exp(LOW_CAP))
            low = low * low
            row_hi[rows, :] += high[:, :ROWS] + high[:, ROWS:]
            row_lo[rows, :] += low[:, :ROWS] + low[:, ROWS:]
            return (
                sums[0] + jnp.sum(high.reshape(WIDE // 8, 8, WIDE), axis=0),
                sums[1] + jnp.sum(low.reshape(WIDE // 8, 8, WIDE), axis=0),
            )

        zero = jnp.zeros((8, WIDE), f32)
        high, low = lax.fori_loop(0, sheet * ROWS // WIDE, rows_step, (zero, zero))
        high = jnp.sum(high, axis=0, keepdims=True)
        low = jnp.sum(low, axis=0, keepdims=True)
        for j in range(WIDE // ROWS):
            at = n * (WIDE // ROWS) + j
            col_all[z, pl.ds(at, 1), :] = high[:, j * ROWS : (j + 1) * ROWS]
            col_all[z, pl.ds(8 + at, 1), :] = low[:, j * ROWS : (j + 1) * ROWS]

    def half_factor(total):
        high, low = total[0:8], total[8:16]
        small = low < math.exp(LOW_LIMIT)
        lse = jnp.where(small, jnp.log(low) - 2 * LOW_SHIFT, jnp.log(high) + 2 * HIGH_SHIFT)
        return jnp.exp(lse * -0.5) * math.sqrt(0.5)

    def weigh(tile):
        lanes = pl.ds(pl.multiple_of(tile * ROWS, ROWS), ROWS)

        def rows_step(m, carry):
            rows = pl.ds(pl.multiple_of(m * WIDE, WIDE), WIDE)
            root = probs[rows, lanes]
            by_row = root * alpha[rows, :]
            by_col = root * beta[pl.ds(tile, 1), :]
            weights[rows, lanes] = (by_row * by_row + by_col * by_col).astype(bf16)
            return carry

        lax.fori_loop(0, sheet * ROWS // WIDE, rows_step, 0)

    def text_part(j):
        flip[...] = weights[:, full(turn(z, j, nz))].T

        @pl.loop(0, geo.width // WIDE)
        def _(n):
            lanes = pl.ds(pl.multiple_of(n * WIDE, WIDE), WIDE)
            gz[j, :, lanes] = dot(flip[...], ia[:, lanes])

    def image_part(q, j):
        rows = full((yh if q else hy) * nx + turn(x, j, nx))

        @pl.loop(0, geo.width // WIDE)
        def _(n):
            lanes = pl.ds(pl.multiple_of(n * WIDE, WIDE), WIDE)
            gx[q * nx + j, :, lanes] = dot(weights[rows, :], ta[:, lanes])

    def ring_rows(d, k):
        part = (k % 2) ^ d
        return slice(part * PART, (part + 1) * PART)

    def ring_target(d, k, size):
        away = size // 2 - (k + 1) // 2
        return (sign(d) * away) % size

    def z_reduce(d, k):
        value = gz[ring_target(d, k, nz), ring_rows(d, k), :]
        if k >= 2:
            arrived(zin.at[d, k - 2], zrs_s.at[d, k - 2], zrs_r.at[d, k - 2])
            value = value + zin[d, k - 2].astype(f32)
        zout[d, k] = value.astype(bf16)
        to = place(turn(z, sign(d), nz), yh, x)
        start(zout.at[d, k], zin.at[d, k], zrs_s.at[d, k], zrs_r.at[d, k], to)

    def x_reduce(q, d, k):
        value = gx[q * nx + ring_target(d, k, nx), ring_rows(d, k), :]
        if k >= 2:
            arrived(xin.at[q, d, k - 2], xrs_s.at[q, d, k - 2], xrs_r.at[q, d, k - 2])
            value = value + xin[q, d, k - 2].astype(f32)
        xout[q, d, k] = value.astype(bf16)
        to = place(z, yh, turn(x, sign(d), nx))
        start(xout.at[q, d, k], xin.at[q, d, k], xrs_s.at[q, d, k], xrs_r.at[q, d, k], to)

    def ring_last(size):
        return [k for k in (size - 3, size - 2) if k >= 0]

    def x_total(q, c):
        value = gx[q * nx, c * PART : (c + 1) * PART, :]
        for d in range(2):
            for k in ring_last(nx):
                if (k % 2) ^ d == c:
                    arrived(xin.at[q, d, k], xrs_s.at[q, d, k], xrs_r.at[q, d, k])
                    value = value + xin[q, d, k].astype(f32)
        return value

    def z_total(c):
        value = gz[0, c * PART : (c + 1) * PART, :]
        for d in range(2):
            for k in ring_last(nz):
                if (k % 2) ^ d == c:
                    arrived(zin.at[d, k], zrs_s.at[d, k], zrs_r.at[d, k])
                    value = value + zin[d, k].astype(f32)
        return value

    def finish(total, other, unit, inverse, out, c):
        rows = slice(c * PART, (c + 1) * PART)
        grad = scale_ref[0] * (total - other.astype(f32))
        along = jnp.sum(grad * unit[rows, :], axis=-1, keepdims=True)
        out[rows, :] = (inverse[rows, :] * (grad - along * unit[rows, :])).astype(bf16)

    both = range(2)
    kz, kx = nz - 1, nx - 1
    for k in range(min(2, kz)):
        for d in both:
            z_gather(d, k)
    for k in range(min(2, kx)):
        for d in both:
            x_gather(0, d, k)
    for c in both:
        y_gather(c)
    mate_send()

    def z_step(k):
        if k < kz:
            for d in both:
                z_gathered(d, k)
            if k + 2 < kz:
                for d in both:
                    z_gather(d, k + 2)

    def x_step(q, k):
        if k < kx:
            for d in both:
                x_gathered(q, d, k)
            if k + 2 < kx:
                for d in both:
                    x_gather(q, d, k + 2)

    z_step(0)
    x_step(0, 0)
    mate_sum()
    y_send()
    z_step(1)
    for c in both:
        y_gathered(c)
        for k in range(min(2, kx)):
            for d in both:
                if (k % 2) ^ d == c:
                    x_gather(1, d, k)
    z_step(2)
    x_step(0, 1)
    x_step(0, 2)
    y_sum()
    x_send()
    z_step(3)
    x_step(1, 0)
    z_step(4)
    x_sum()
    z_send()
    for k in range(1, kx):
        x_step(1, k)
    for k in range(5, kz - 1):
        z_step(k)

    @pl.loop(0, blocks - 1)
    def _(i):
        logits_block(lax.rem(late + 1 + i, blocks))

    if kz - 1 >= 5:
        z_step(kz - 1)
    logits_block(late)
    for m in range(sheet):
        rows = slice(m * ROWS, (m + 1) * ROWS)
        row_all[b, m : m + 1, :] = jnp.sum(row_hi[rows, :].T, axis=0, keepdims=True)
        row_all[b, 8 + m : 9 + m, :] = jnp.sum(row_lo[rows, :].T, axis=0, keepdims=True)
    for o in range(1, nz):
        start(col_all.at[z], col_all.at[z], col_s.at[o], col_r.at[o], place(turn(z, o, nz), yh, x))
    for q in both:
        for o in range(nx):
            if q or o:
                i = q * nx + o
                to = place(z, hy if q else yh, turn(x, o, nx))
                start(row_all.at[b], row_all.at[b], row_s.at[i], row_r.at[i], to)
    z_sum()
    x_spread()
    for o in range(1, nz):
        arrived(col_all.at[turn(z, -o, nz)], col_s.at[o], col_r.at[o])
    total = col_all[0]
    for o in range(1, nz):
        total = total + col_all[o]
    beta[...] = half_factor(total)
    for q in both:
        for o in range(nx):
            if q or o:
                i = q * nx + o
                arrived(row_all.at[(hy if q else yh) * nx + turn(x, -o, nx)], row_s.at[i], row_r.at[i])
    total = row_all[0]
    for o in range(1, sheet):
        total = total + row_all[o]
    factor = half_factor(total)
    for m in range(sheet):
        rows = slice(m * ROWS, (m + 1) * ROWS)
        alpha[rows, :] = jnp.broadcast_to(factor[m : m + 1, :], (ROWS, ROWS)).T

    weigh(turn(z, nz // 2, nz))
    text_part(nz // 2)
    for d in both:
        z_reduce(d, 0)

    @pl.loop(0, nz - 1)
    def _(i):
        weigh(turn(z, nz // 2 + 1 + i, 2 * nz) % nz)

    def z_stage(k):
        if k < kz:
            for d in both:
                z_reduce(d, k)

    def x_stage(q, k):
        if k < kx:
            for d in both:
                x_reduce(q, d, k)

    def text_parts(away):
        if 0 < away < nz // 2:
            text_part(away)
            text_part(nz - away)

    def image_parts(q, away):
        if 0 < away < nx // 2:
            image_part(q, away)
            image_part(q, nx - away)

    image_part(0, nx // 2)
    x_stage(0, 0)
    text_parts(nz // 2 - 1)
    z_stage(1)
    image_parts(0, nx // 2 - 1)
    x_stage(0, 1)
    x_spread_done()
    y_spread()
    z_stage(2)
    x_stage(0, 2)
    image_part(0, 0)
    image_part(1, nx // 2)
    x_stage(1, 0)
    text_parts(nz // 2 - 2)
    z_stage(3)
    image_parts(1, nx // 2 - 1)
    x_stage(1, 1)
    for c in both:
        yout[c] = x_total(0, c).astype(bf16)
        start(yout.at[c], yin.at[c], yrs_s.at[c], yrs_r.at[c], facing)
    z_stage(4)
    x_stage(1, 2)
    y_spread_done()
    mate_spread()
    text_parts(nz // 2 - 3)
    z_stage(5)
    z_stage(6)
    image_part(1, 0)
    text_part(0)
    mate_spread_done()
    for row in range(KS):
        for t in range(TILES):
            kg_ref[row, :, t * LANES : (t + 1) * LANES] = fin[
                pl.ds(row * KS * TILES + t, KS, stride=TILES), :
            ]
    for t in range(TILES):
        cg_ref[:, t * LANES : (t + 1) * LANES] = fin[pl.ds(SPOTS * TILES + t, 3, stride=TILES), :]
    for c in both:
        value = x_total(1, c)
        arrived(yin.at[c], yrs_s.at[c], yrs_r.at[c])
        finish(value + yin[c].astype(f32), ta[slot(z, c), :], ui, vi, ig_ref, c)
    for c in both:
        finish(z_total(c), ia[slot(b, c), :], ut, vt, tg_ref, c)
    for moving in sent:
        moving.wait_send()


def loss_block(geo, scale, image_rows, text_rows, terms):
    f32, bf16 = jnp.float32, jnp.bfloat16
    vmem = pltpu.VMEM
    dma = pltpu.SemaphoreType.DMA
    images, texts, width = geo.sheet * ROWS, geo.z * ROWS, geo.width
    kz, kx = geo.z - 1, geo.x - 1
    scratch = [
        vmem((images, width), bf16), vmem((texts, width), bf16),
        vmem((ROWS, width), f32), vmem((ROWS, width), f32), vmem((ROWS, 1), f32), vmem((ROWS, 1), f32),
        vmem((images, texts), f32), vmem((images, texts), bf16), vmem((ROWS, images), bf16),
        vmem((images, ROWS), f32), vmem((images, ROWS), f32), vmem((images, ROWS), f32), vmem((8, ROWS), f32),
        vmem((geo.sheet, 16, ROWS), f32), vmem((geo.z, 16, ROWS), f32),
        vmem((geo.z, ROWS, width), f32), vmem((2 * geo.x, ROWS, width), f32),
        vmem((2, kz, PART, width), bf16), vmem((2, kz, PART, width), bf16),
        vmem((2, 2, kx, PART, width), bf16), vmem((2, 2, kx, PART, width), bf16),
        vmem((2, PART, width), bf16), vmem((2, PART, width), bf16),
        vmem((geo.half, LANES), f32), vmem((geo.half, LANES), f32),
        vmem((geo.y, geo.y_rows, LANES), f32), vmem((geo.y_rows, LANES), f32),
        vmem((geo.x, geo.x_rows, LANES), f32), vmem((geo.z, geo.x_rows, LANES), f32), vmem((SLACK, LANES), f32),
        dma((2, kz)), dma((2, kz)), dma((2, 2, kx)), dma((2, 2, kx)), dma((2,)), dma((2,)),
        dma((geo.sheet,)), dma((geo.sheet,)), dma((geo.z,)), dma((geo.z,)),
        dma((2, kz)), dma((2, kz)), dma((2, 2, kx)), dma((2, 2, kx)), dma((2,)), dma((2,)),
        dma((1,)), dma((1,)), dma((geo.y,)), dma((geo.y,)), dma((geo.x,)), dma((geo.x,)), dma((geo.z,)), dma((geo.z,)),
        dma((geo.x,)), dma((geo.x,)), dma((geo.y,)), dma((geo.y,)), dma((1,)), dma((1,)),
    ]
    return pl.pallas_call(
        functools.partial(loss_kernel, geo),
        out_shape=(
            jax.ShapeDtypeStruct((ROWS, width), bf16),
            jax.ShapeDtypeStruct((ROWS, width), bf16),
            jax.ShapeDtypeStruct((KS, KS, TILES * LANES), f32),
            jax.ShapeDtypeStruct((3, TILES * LANES), f32),
        ),
        in_specs=[pl.BlockSpec(memory_space=pltpu.SMEM)] + [pl.BlockSpec(memory_space=pltpu.VMEM)] * 3,
        out_specs=[pl.BlockSpec(memory_space=pltpu.VMEM)] * 4,
        scratch_shapes=scratch,
        compiler_params=pltpu.CompilerParams(
            collective_id=0, has_side_effects=True, vmem_limit_bytes=52 << 20
        ),
    )(scale.reshape(1), image_rows, text_rows, terms)


def per_device(
    geo, image_embed, text_embed, logit_scale, block_input, dw_kernel, dw_bias, ln_gain, block_grad
):
    d_input, terms = conv_block(block_input[0], block_grad[0], dw_kernel, dw_bias, ln_gain)
    image_grad, text_grad, kernel_grad, channel_grads = loss_block(
        geo, logit_scale, image_embed[0], text_embed[0], terms
    )
    return (image_grad[None], text_grad[None], d_input[None], kernel_grad, channel_grads)


def solution(mesh, geo=None):
    geo = geo or Geometry(8, 2, 4, 2, 2, 1024)
    placed = (
        P("grp", "blk", None),
        P("grp", "blk", None),
        P(),
        P(("blk", "grp"), None, None, None),
        P(),
        P(),
        P(),
        P(("blk", "grp"), None, None, None),
    )
    return jax.shard_map(
        functools.partial(per_device, geo),
        mesh=mesh,
        in_specs=placed,
        out_specs=(
            P("grp", "blk", None),
            P("grp", "blk", None),
            P(("blk", "grp"), None, None, None),
            P(),
            P(),
        ),
        check_vma=False,
    )
```

time: 322 us -> 86.2 us (0.27)
  waiting for transfers between devices: 202 us -> 0 us
  Pallas kernels: 5.47 us -> 77.7 us
  blocking collectives: 58.9 us -> 0 us
  matrix products: 16.1 us -> 0 us
  other arithmetic: 16.1 us -> 0 us
  between operations: 16 us -> 1.34 us
    psum x1 -> x0, waiting for transfers between devices: 97.2 us -> none  [per_device(): totals = lax.psum(jnp.concatenate([kterm, cterm], axis=0), ('blk', 'grp'))]
    all_gather x2 -> x0, waiting for transfers between devices: 92.4 us -> none  [the longest x1 49 us: per_device(): lax.all_gather(hat_image, 'blk', axis=0, tiled=True, axis_index_groups=sh...]
    pallas_call x0 -> x1, Pallas kernels: none -> 72.2 us  [loss_block(): pl.pallas_call(functools.partial(loss_kernel, geo), out_shape=(jax.ShapeD...]
    all_gather x2 -> x0, blocking collectives: 58.9 us -> none  [lse_over(): lax.all_gather(jnp.stack([peak, mass]), 'blk', axis_index_groups=groups)]
    dot_general x3 -> x0, matrix products: 16.1 us -> none  [contract(): lax.dot_general(left, right, ((dims[0], dims[1]), ((), ())), preferred_el...]
    reduce_scatter x2 -> x0, waiting for transfers between devices: 12.5 us -> none  [the longest x1 12.5 us: per_device(): lax.psum_scatter(part_image, 'blk', axis_index_groups=sheets, tiled=True)]
    reduce_sum x8 -> x0, other arithmetic: 6.51 us -> none  [the longest x2 2.52 us: project_back(): along = jnp.sum(grad_hat * unit_hat, axis=-1, keepdims=True)]
    broadcast_in_dim x2 -> x0, other arithmetic: 3.92 us -> none  [the longest x1 1.97 us: per_device(): text_grad[None]]
  transfers between devices with their start and end apart: 5 -> 0, of which waited for: 4 -> 0; matrix products, arithmetic and copies ran while one was open for 9% -> 0% of each run, Pallas kernels for 2% -> 0%
where the time goes in v2:
time: 86.2 us; the launch traced here: 85.5 us
  Pallas kernels  77.7 us (90%)
  local copies, waits for them, and re-layouts  6.54 us (8%)
  between operations  1.34 us (2%)
    pallas_call x1, Pallas kernels, loss_block(): pl.pallas_call(functools.partial(loss_kernel, geo), out_shape=(jax.ShapeD...  72.2 us
    unnamed x20, local copies, waits for them, and re-layouts  6.52 us
    pallas_call x1, Pallas kernels, conv_block(): pl.pallas_call(conv_kernel, out_shape=(jax.ShapeDtypeStruct((GRID, GRID,...  5.47 us

profile of v2, /device:TPU:8, one launch (start us, length us, event | category | flops | bytes accessed | tf_op | source)
XLA Modules:
  0.0 85.5 jit_solution(6404996371682461397)
XLA Ops:
  0.6 0.0 copy-start.6
  1.3 0.0 copy-done.6
  1.3 0.0 copy-start.7
  1.3 0.7 copy-done.7
  2.0 0.0 copy-start
  2.0 1.0 %copy-done = bf16[1,7,7,3072]{3,2,1,0:T(8,128)(2,1)S(1)} copy-done((bf16[1,7,7,3072]{3,2,1,0:T(8,128)(2,1)S(1)}, bf16[1,7,7,3072]{3,2,1,0:T(8,128)(2,1)}, u32[]{:S(2)}) %copy-start) | copy-done | bytes 301080
  3.0 0.0 copy-start.1
  3.0 1.0 %copy-done.1 = bf16[1,7,7,3072]{3,2,1,0:T(8,128)(2,1)S(1)} copy-done((bf16[1,7,7,3072]{3,2,1,0:T(8,128)(2,1)S(1)}, bf16[1,7,7,3072]{3,2,1,0:T(8,128)(2,1)}, u32[]{:S(2)}) %copy-start.1) | copy-done | bytes 301080
  4.0 0.0 copy-start.2
  4.0 1.0 %copy-done.2 = bf16[7,7,3072]{2,1,0:T(8,128)(2,1)S(1)} copy-done((bf16[7,7,3072]{2,1,0:T(8,128)(2,1)S(1)}, bf16[7,7,3072]{2,1,0:T(8,128)(2,1)}, u32[]{:S(2)}) %copy-start.2) | copy-done | bytes 301080
  5.0 0.0 copy-start.3
  5.0 0.0 copy-start.4
  5.0 5.5 %shard_map.119 = (bf16[7,7,3072]{2,1,0:T(8,128)(2,1)}, f32[1280,128]{1,0:T(8,128)S(1)}) custom-call(bf16[7,7,3072]{2,1,0:T(8,128)(2,1)S(1)} %bitcast.9, bf16[7,7,3072]{2,1,0:T(8,128)(2,1)S(1)} %bitcast.10, bf16[7,7,3072]{2,1,0:T(8,128)(2,1)S(1)} %copy-done.2, bf16[1,3072]{1,0:T(2,128)(2,1)S(1)} %reshape.20.bias_ref, bf16[1,3072]{1,0:T(2,128)(2,1)S(1)} %reshape.21.gain_ref), custom_call_target="tpu_custom_call" | custom-call | flops 30000000 | bytes 2500000 | tf_op jit(solution)/shard_map/pallas_call | solution.py:132
  10.4 0.0 copy-done.3
  10.4 0.0 copy-done.4
  10.4 72.2 %shard_map.120 = (bf16[128,1024]{1,0:T(8,128)(2,1)S(1)}, bf16[128,1024]{1,0:T(8,128)(2,1)S(1)}, f32[7,7,3072]{2,1,0:T(8,128)}, f32[3,3072]{1,0:T(4,128)S(1)}) custom-call(f32[1]{0:T(128)} %bitcast.8.scale_ref, bf16[128,1024]{1,0:T(8,128)(2,1)S(1)} %bitcast.13, bf16[128,1024]{1,0:T(8,128)(2,1)S(1)} %bitcast.14, f32[1280,128]{1,0:T(8,128)S(1)} %get-tuple-element.11.terms_ref), custom_call_target="tpu_custom_call" | custom-call | tf_op jit(solution)/shard_map/pallas_call | solution.py:667
  82.7 0.0 copy-start.5
  82.7 0.7 copy.18
  83.4 0.7 copy.19
  84.1 0.0 copy-done.5
  84.1 0.8 copy.20
  84.9 0.6 copy.21
  (2 shorter events, 0.0 us)
Async XLA Ops:
  0.6 0.7 copy-start.6
  1.3 0.7 copy-start.7
  2.0 1.0 %copy-start = (bf16[1,7,7,3072]{3,2,1,0:T(8,128)(2,1)S(1)}, bf16[1,7,7,3072]{3,2,1,0:T(8,128)(2,1)}, u32[]{:S(2)}) copy-start(bf16[1,7,7,3072]{3,2,1,0:T(8,128)(2,1)} %param.11) | copy-start | bytes 903172
  3.0 1.0 %copy-start.1 = (bf16[1,7,7,3072]{3,2,1,0:T(8,128)(2,1)S(1)}, bf16[1,7,7,3072]{3,2,1,0:T(8,128)(2,1)}, u32[]{:S(2)}) copy-start(bf16[1,7,7,3072]{3,2,1,0:T(8,128)(2,1)} %param.15) | copy-start | bytes 903172
  4.0 1.0 %copy-start.2 = (bf16[7,7,3072]{2,1,0:T(8,128)(2,1)S(1)}, bf16[7,7,3072]{2,1,0:T(8,128)(2,1)}, u32[]{:S(2)}) copy-start(bf16[7,7,3072]{2,1,0:T(8,128)(2,1)} %k_ref.1) | copy-start | bytes 903172
  5.0 5.5 %copy-start.3 = (bf16[1,128,1024]{2,1,0:T(8,128)(2,1)S(1)}, bf16[1,128,1024]{2,1,0:T(8,128)(2,1)}, u32[]{:S(2)}) copy-start(bf16[1,128,1024]{2,1,0:T(8,128)(2,1)} %param.8) | copy-start | bytes 786436
  5.0 5.5 %copy-start.4 = (bf16[1,128,1024]{2,1,0:T(8,128)(2,1)S(1)}, bf16[1,128,1024]{2,1,0:T(8,128)(2,1)}, u32[]{:S(2)}) copy-start(bf16[1,128,1024]{2,1,0:T(8,128)(2,1)} %param.9) | copy-start | bytes 786436
  82.7 1.4 %copy-start.5 = (f32[7,7,3072]{2,1,0:T(8,128)S(1)}, f32[7,7,3072]{2,1,0:T(8,128)}, u32[]{:S(2)}) copy-start(f32[7,7,3072]{2,1,0:T(8,128)} %get-tuple-element.25) | copy-start | bytes 1806340

commit v3 on v2

--- a/solution.py
+++ b/solution.py
@@ -23,7 +23,7 @@
     return jnp.sum(folded, axis=2, keepdims=True) * (1.0 / count)
 
 
-def conv_kernel(x_ref, g_ref, k_ref, bias_ref, gain_ref, din_ref, terms_ref, xs, gs, ks, cs, ds, bs):
+def conv_terms(x_ref, g_ref, k_ref, bias_ref, gain_ref, din_ref, terms_ref, xs, gs, ks, cs, ds, bs):
     channels = TILES * LANES
 
     def spread(src, dst):
@@ -36,9 +36,8 @@
     spread(x_ref, xs)
     spread(k_ref, ks)
     spread(g_ref, gs)
-    for t in range(TILES):
-        bs[t : t + 1, :] = bias_ref[0:1, t * LANES : (t + 1) * LANES].astype(jnp.float32)
-        bs[TILES + t : TILES + t + 1, :] = gain_ref[0:1, t * LANES : (t + 1) * LANES].astype(jnp.float32)
+    bs[0:TILES, :] = bias_ref[...].astype(jnp.float32).reshape(TILES, LANES)
+    bs[TILES : 2 * TILES, :] = gain_ref[...].astype(jnp.float32).reshape(TILES, LANES)
 
     def rows(part, spot):
         return pl.ds(pl.multiple_of(spot * TILES + part * 8, 8), 8)
@@ -126,23 +125,6 @@
             ].astype(jnp.bfloat16)
 
 
-def conv_block(x, g, k, bias, gain):
-    f32 = jnp.float32
-    big = pltpu.VMEM((SPOTS * TILES, LANES), f32)
-    return pl.pallas_call(
-        conv_kernel,
-        out_shape=(
-            jax.ShapeDtypeStruct((GRID, GRID, TILES * LANES), jnp.bfloat16),
-            jax.ShapeDtypeStruct((SLACK, LANES), f32),
-        ),
-        in_specs=[pl.BlockSpec(memory_space=pltpu.VMEM)] * 5,
-        out_specs=[pl.BlockSpec(memory_space=pltpu.VMEM)] * 2,
-        scratch_shapes=[big, big, big, big, big, pltpu.VMEM((2 * TILES, LANES), f32)],
-        compiler_params=pltpu.CompilerParams(vmem_limit_bytes=24 << 20),
-        cost_estimate=pl.CostEstimate(flops=30_000_000, bytes_accessed=2_500_000, transcendentals=49),
-    )(x, g, k, bias.reshape(1, -1), gain.reshape(1, -1))
-
-
 ROWS = 128
 PART = 64
 WIDE = 256
@@ -169,7 +151,9 @@
 
 
 def loss_kernel(
-    geo, scale_ref, img_ref, txt_ref, terms_ref, ig_ref, tg_ref, kg_ref, cg_ref,
+    geo, scale_ref, img_hbm, txt_hbm, x_hbm, g_hbm, k_hbm, bias_hbm, gain_hbm,
+    ig_ref, tg_ref, cg_ref, din_hbm, kg_hbm,
+    din_ref, kg_ref, img_ref, txt_ref, x_ref, g_ref, k_ref, bias_ref, gain_ref, terms_ref, xs, gs, ks, cs, ds, bs, load_sem,
     ia, ta, ui, ut, vi, vt, probs, weights, flip, row_hi, row_lo, alpha, beta, row_all, col_all, gz, gx,
     zout, zin, xout, xin, yout, yin, l1, hsum, l2, qsum, l3, l4, fin,
     zag_s, zag_r, xag_s, xag_r, yag_s, yag_r, row_s, row_r, col_s, col_r,
@@ -226,6 +210,13 @@
     peers.append(mate)
     for peer in peers:
         pl.semaphore_signal(barrier, inc=1, device_id=peer, device_id_type=MESH)
+    operands = (txt_hbm, img_hbm, x_hbm, k_hbm, g_hbm, bias_hbm, gain_hbm)
+    held = (txt_ref, img_ref, x_ref, k_ref, g_ref, bias_ref, gain_ref)
+    loads = [
+        pltpu.make_async_copy(src, dst, load_sem.at[i]) for i, (src, dst) in enumerate(zip(operands, held))
+    ]
+    for load in loads:
+        load.start()
 
     def slot(index, part):
         return pl.ds(pl.multiple_of(index * ROWS + part * PART, PART), PART)
@@ -241,7 +232,9 @@
         inverse[...] = inv
         everyone[full(index), :] = scaled.astype(bf16)
 
+    loads[0].wait()
     unit_rows(txt_ref, ut, vt, ta, z)
+    loads[1].wait()
     unit_rows(img_ref, ui, vi, ia, b)
     pl.semaphore_wait(barrier, len(peers))
 
@@ -479,6 +472,11 @@
             x_gather(0, d, k)
     for c in both:
         y_gather(c)
+    for load in loads[2:]:
+        load.wait()
+    conv_terms(x_ref, g_ref, k_ref, bias_ref, gain_ref, din_ref, terms_ref, xs, gs, ks, cs, ds, bs)
+    din_out = pltpu.make_async_copy(din_ref, din_hbm, load_sem.at[len(loads)])
+    din_out.start()
     mate_send()
 
     def z_step(k):
@@ -499,8 +497,6 @@
 
     z_step(0)
     x_step(0, 0)
-    mate_sum()
-    y_send()
     z_step(1)
     for c in both:
         y_gathered(c)
@@ -508,8 +504,10 @@
             for d in both:
                 if (k % 2) ^ d == c:
                     x_gather(1, d, k)
+    mate_sum()
+    y_send()
+    x_step(0, 1)
     z_step(2)
-    x_step(0, 1)
     x_step(0, 2)
     y_sum()
     x_send()
@@ -517,7 +515,6 @@
     x_step(1, 0)
     z_step(4)
     x_sum()
-    z_send()
     for k in range(1, kx):
         x_step(1, k)
     for k in range(5, kz - 1):
@@ -529,6 +526,7 @@
 
     if kz - 1 >= 5:
         z_step(kz - 1)
+    z_send()
     logits_block(late)
     for m in range(sheet):
         rows = slice(m * ROWS, (m + 1) * ROWS)
@@ -563,15 +561,6 @@
         rows = slice(m * ROWS, (m + 1) * ROWS)
         alpha[rows, :] = jnp.broadcast_to(factor[m : m + 1, :], (ROWS, ROWS)).T
 
-    weigh(turn(z, nz // 2, nz))
-    text_part(nz // 2)
-    for d in both:
-        z_reduce(d, 0)
-
-    @pl.loop(0, nz - 1)
-    def _(i):
-        weigh(turn(z, nz // 2 + 1 + i, 2 * nz) % nz)
-
     def z_stage(k):
         if k < kz:
             for d in both:
@@ -592,32 +581,45 @@
             image_part(q, away)
             image_part(q, nx - away)
 
+    half = nz // 2
+    weigh(turn(z, half, nz))
+    text_part(half)
+    z_stage(0)
+    if half > 1:
+        weigh(turn(z, half - 1, nz))
+        weigh(turn(z, -(half - 1), nz))
+    text_parts(half - 1)
+    z_stage(1)
+    first = max(half - 1, 1)
+
+    @pl.loop(0, 2 * first - 1)
+    def _(i):
+        weigh(turn(z, i - (first - 1), nz))
+
     image_part(0, nx // 2)
     x_stage(0, 0)
-    text_parts(nz // 2 - 1)
-    z_stage(1)
     image_parts(0, nx // 2 - 1)
     x_stage(0, 1)
     x_spread_done()
     y_spread()
+    image_part(1, nx // 2)
     z_stage(2)
+    image_parts(1, nx // 2 - 1)
     x_stage(0, 2)
+    x_stage(1, 0)
+    x_stage(1, 1)
+    text_parts(half - 2)
+    z_stage(3)
     image_part(0, 0)
-    image_part(1, nx // 2)
-    x_stage(1, 0)
-    text_parts(nz // 2 - 2)
-    z_stage(3)
-    image_parts(1, nx // 2 - 1)
-    x_stage(1, 1)
+    z_stage(4)
     for c in both:
         yout[c] = x_total(0, c).astype(bf16)
         start(yout.at[c], yin.at[c], yrs_s.at[c], yrs_r.at[c], facing)
-    z_stage(4)
+    text_parts(half - 3)
+    z_stage(5)
     x_stage(1, 2)
     y_spread_done()
     mate_spread()
-    text_parts(nz // 2 - 3)
-    z_stage(5)
     z_stage(6)
     image_part(1, 0)
     text_part(0)
@@ -629,23 +631,32 @@
             ]
     for t in range(TILES):
         cg_ref[:, t * LANES : (t + 1) * LANES] = fin[pl.ds(SPOTS * TILES + t, 3, stride=TILES), :]
+    kg_out = pltpu.make_async_copy(kg_ref, kg_hbm, load_sem.at[len(loads) + 1])
+    kg_out.start()
     for c in both:
         value = x_total(1, c)
         arrived(yin.at[c], yrs_s.at[c], yrs_r.at[c])
         finish(value + yin[c].astype(f32), ta[slot(z, c), :], ui, vi, ig_ref, c)
     for c in both:
         finish(z_total(c), ia[slot(b, c), :], ut, vt, tg_ref, c)
+    din_out.wait()
+    kg_out.wait()
     for moving in sent:
         moving.wait_send()
 
 
-def loss_block(geo, scale, image_rows, text_rows, terms):
+def loss_block(geo, scale, image_rows, text_rows, x, g, k, bias, gain):
     f32, bf16 = jnp.float32, jnp.bfloat16
     vmem = pltpu.VMEM
     dma = pltpu.SemaphoreType.DMA
     images, texts, width = geo.sheet * ROWS, geo.z * ROWS, geo.width
     kz, kx = geo.z - 1, geo.x - 1
+    big = vmem((SPOTS * TILES, LANES), f32)
+    maps = vmem((GRID, GRID, TILES * LANES), bf16)
     scratch = [
+        maps, vmem((KS, KS, TILES * LANES), f32), vmem((ROWS, width), bf16), vmem((ROWS, width), bf16), maps, maps, maps,
+        vmem((TILES * LANES,), bf16), vmem((TILES * LANES,), bf16), vmem((SLACK, LANES), f32),
+        big, big, big, big, big, vmem((2 * TILES, LANES), f32), dma((9,)),
         vmem((images, width), bf16), vmem((texts, width), bf16),
         vmem((ROWS, width), f32), vmem((ROWS, width), f32), vmem((ROWS, 1), f32), vmem((ROWS, 1), f32),
         vmem((images, texts), f32), vmem((images, texts), bf16), vmem((ROWS, images), bf16),
@@ -669,24 +680,49 @@
         out_shape=(
             jax.ShapeDtypeStruct((ROWS, width), bf16),
             jax.ShapeDtypeStruct((ROWS, width), bf16),
+            jax.ShapeDtypeStruct((3, TILES * LANES), f32),
+            jax.ShapeDtypeStruct((GRID, GRID, TILES * LANES), bf16),
             jax.ShapeDtypeStruct((KS, KS, TILES * LANES), f32),
-            jax.ShapeDtypeStruct((3, TILES * LANES), f32),
         ),
-        in_specs=[pl.BlockSpec(memory_space=pltpu.SMEM)] + [pl.BlockSpec(memory_space=pltpu.VMEM)] * 3,
-        out_specs=[pl.BlockSpec(memory_space=pltpu.VMEM)] * 4,
+        in_specs=[pl.BlockSpec(memory_space=pltpu.SMEM)] + [pl.BlockSpec(memory_space=pltpu.HBM)] * 7,
+        out_specs=[pl.BlockSpec(memory_space=pltpu.VMEM)] * 3 + [pl.BlockSpec(memory_space=pltpu.HBM)] * 2,
         scratch_shapes=scratch,
         compiler_params=pltpu.CompilerParams(
-            collective_id=0, has_side_effects=True, vmem_limit_bytes=52 << 20
+            collective_id=0, has_side_effects=True, vmem_limit_bytes=60 << 20
         ),
-    )(scale.reshape(1), image_rows, text_rows, terms)
+    )(scale.reshape(1), image_rows, text_rows, x, g, k, bias, gain)
+
+
+def hand_out_kernel(*refs):
+    count = len(refs) // 2
+    sems = refs[-1]
+    copies = [pltpu.make_async_copy(refs[i], refs[count + i], sems.at[i]) for i in range(count)]
+    for moving in copies:
+        moving.start()
+    for moving in copies:
+        moving.wait()
+
+
+def hand_out(*arrays):
+    anywhere = [pl.BlockSpec(memory_space=pl.ANY)] * 3 + [pl.BlockSpec(memory_space=pltpu.HBM)] * 2
+    return pl.pallas_call(
+        hand_out_kernel,
+        out_shape=tuple(jax.ShapeDtypeStruct(a.shape, a.dtype) for a in arrays),
+        in_specs=anywhere,
+        out_specs=anywhere,
+        scratch_shapes=[pltpu.SemaphoreType.DMA((len(arrays),))],
+        compiler_params=pltpu.CompilerParams(vmem_limit_bytes=60 << 20),
+    )(*arrays)
 
 
 def per_device(
     geo, image_embed, text_embed, logit_scale, block_input, dw_kernel, dw_bias, ln_gain, block_grad
 ):
-    d_input, terms = conv_block(block_input[0], block_grad[0], dw_kernel, dw_bias, ln_gain)
-    image_grad, text_grad, kernel_grad, channel_grads = loss_block(
-        geo, logit_scale, image_embed[0], text_embed[0], terms
+    image_grad, text_grad, channel_grads, d_input, kernel_grad = hand_out(
+        *loss_block(
+            geo, logit_scale, image_embed[0], text_embed[0],
+            block_input[0], block_grad[0], dw_kernel, dw_bias, ln_gain,
+        )
     )
     return (image_grad[None], text_grad[None], d_input[None], kernel_grad, channel_grads)
 

time: 86.2 us -> 122 us (1.42)
  Pallas kernels: 77.7 us -> 121 us
  local copies, waits for them, and re-layouts: 6.54 us -> 0 us
    pallas_call x1, Pallas kernels: 5.47 us -> 49.8 us  [hand_out(): pl.pallas_call(hand_out_kernel, out_shape=tuple((jax.ShapeDtypeStruct(a.s...]
    unnamed x20 -> x0, local copies, waits for them, and re-layouts: 6.52 us -> none
where the time goes in v3:
time: 122 us
  Pallas kernels  121 us (99%)
  between operations  1.29 us (1%)
    pallas_call x1, Pallas kernels, loss_block(): pl.pallas_call(functools.partial(loss_kernel, geo), out_shape=(jax.ShapeD...  71.1 us
    pallas_call x1, Pallas kernels, hand_out(): pl.pallas_call(hand_out_kernel, out_shape=tuple((jax.ShapeDtypeStruct(a.s...  49.8 us

profile of v3, /device:TPU:8, one launch (start us, length us, event | category | flops | bytes accessed | tf_op | source)
XLA Modules:
  0.0 122.2 jit_solution(9550545657076226336)
XLA Ops:
  1.3 71.1 %shard_map.119 = (bf16[128,1024]{1,0:T(8,128)(2,1)}, bf16[128,1024]{1,0:T(8,128)(2,1)}, f32[3,3072]{1,0:T(4,128)}, bf16[7,7,3072]{2,1,0:T(8,128)(2,1)}, f32[7,7,3072]{2,1,0:T(8,128)}) custom-call(f32[1]{0:T(128)} %bitcast.8.scale_ref, bf16[128,1024]{1,0:T(8,128)(2,1)} %bitcast.11, bf16[128,1024]{1,0:T(8,128)(2,1)} %bitcast.12, bf16[7,7,3072]{2,1,0:T(8,128)(2,1)} %bitcast.9, ...), custom_call_target="tpu_custom_call" | custom-call | tf_op jit(solution)/shard_map/pallas_call | solution.py:678
  72.4 49.8 %shard_map.120 = (bf16[128,1024]{1,0:T(8,128)(2,1)}, bf16[128,1024]{1,0:T(8,128)(2,1)}, f32[3,3072]{1,0:T(4,128)}, bf16[7,7,3072]{2,1,0:T(8,128)(2,1)}, f32[7,7,3072]{2,1,0:T(8,128)}) custom-call(bf16[128,1024]{1,0:T(8,128)(2,1)} %get-tuple-element.15.refs_0_, bf16[128,1024]{1,0:T(8,128)(2,1)} %get-tuple-element.16.refs_1_, ...), custom_call_target="tpu_custom_call" | custom-call | tf_op jit(solution)/shard_map/pallas_call | solution.py:708

commit v4 on v3

--- a/solution.py
+++ b/solution.py
@@ -694,23 +694,28 @@
 
 
 def hand_out_kernel(*refs):
-    count = len(refs) // 2
-    sems = refs[-1]
-    copies = [pltpu.make_async_copy(refs[i], refs[count + i], sems.at[i]) for i in range(count)]
-    for moving in copies:
+    count = (len(refs) - 2) // 3
+    into, away = refs[-2], refs[-1]
+    loads = [pltpu.make_async_copy(refs[i], refs[2 * count + i], into.at[i]) for i in range(count)]
+    stores = [pltpu.make_async_copy(refs[2 * count + i], refs[count + i], away.at[i]) for i in range(count)]
+    for moving in loads:
         moving.start()
-    for moving in copies:
+    for load, store in zip(loads, stores):
+        load.wait()
+        store.start()
+    for moving in stores:
         moving.wait()
 
 
 def hand_out(*arrays):
-    anywhere = [pl.BlockSpec(memory_space=pl.ANY)] * 3 + [pl.BlockSpec(memory_space=pltpu.HBM)] * 2
+    held = [pl.BlockSpec(memory_space=pltpu.HBM)] * len(arrays)
+    sems = pltpu.SemaphoreType.DMA((len(arrays),))
     return pl.pallas_call(
         hand_out_kernel,
         out_shape=tuple(jax.ShapeDtypeStruct(a.shape, a.dtype) for a in arrays),
-        in_specs=anywhere,
-        out_specs=anywhere,
-        scratch_shapes=[pltpu.SemaphoreType.DMA((len(arrays),))],
+        in_specs=held,
+        out_specs=held,
+        scratch_shapes=[pltpu.VMEM(a.shape, a.dtype) for a in arrays] + [sems, sems],
         compiler_params=pltpu.CompilerParams(vmem_limit_bytes=60 << 20),
     )(*arrays)
 

time: 122 us -> 74.9 us (0.61)
  Pallas kernels: 121 us -> 73.4 us
    pallas_call x1, Pallas kernels: 49.8 us -> 2.32 us  [hand_out(): pl.pallas_call(hand_out_kernel, out_shape=tuple((jax.ShapeDtypeStruct(a.s...]
where the time goes in v4:
time: 74.9 us; the launch traced here: 74.7 us
  Pallas kernels  73.4 us (98%)
  between operations  1.29 us (2%)
    pallas_call x1, Pallas kernels, loss_block(): pl.pallas_call(functools.partial(loss_kernel, geo), out_shape=(jax.ShapeD...  71.1 us
    pallas_call x1, Pallas kernels, hand_out(): pl.pallas_call(hand_out_kernel, out_shape=tuple((jax.ShapeDtypeStruct(a.s...  2.32 us

profile of v4, /device:TPU:8, one launch (start us, length us, event | category | flops | bytes accessed | tf_op | source)
XLA Modules:
  0.0 74.7 jit_solution(2378340017874351697)
XLA Ops:
  1.3 71.1 %shard_map.119 = (bf16[128,1024]{1,0:T(8,128)(2,1)}, bf16[128,1024]{1,0:T(8,128)(2,1)}, f32[3,3072]{1,0:T(4,128)}, bf16[7,7,3072]{2,1,0:T(8,128)(2,1)}, f32[7,7,3072]{2,1,0:T(8,128)}) custom-call(f32[1]{0:T(128)} %bitcast.8.scale_ref, bf16[128,1024]{1,0:T(8,128)(2,1)} %bitcast.11, bf16[128,1024]{1,0:T(8,128)(2,1)} %bitcast.12, bf16[7,7,3072]{2,1,0:T(8,128)(2,1)} %bitcast.9, ...), custom_call_target="tpu_custom_call" | custom-call | tf_op jit(solution)/shard_map/pallas_call | solution.py:678
  72.4 2.3 %shard_map.120 = (bf16[128,1024]{1,0:T(8,128)(2,1)}, bf16[128,1024]{1,0:T(8,128)(2,1)}, f32[3,3072]{1,0:T(4,128)}, bf16[7,7,3072]{2,1,0:T(8,128)(2,1)}, f32[7,7,3072]{2,1,0:T(8,128)}) custom-call(bf16[128,1024]{1,0:T(8,128)(2,1)} %get-tuple-element.15.refs_0_, bf16[128,1024]{1,0:T(8,128)(2,1)} %get-tuple-element.16.refs_1_, ...), custom_call_target="tpu_custom_call" | custom-call | tf_op jit(solution)/shard_map/pallas_call | solution.py:713

commit v5 on v4

--- a/solution.py
+++ b/solution.py
@@ -154,7 +154,7 @@
     geo, scale_ref, img_hbm, txt_hbm, x_hbm, g_hbm, k_hbm, bias_hbm, gain_hbm,
     ig_ref, tg_ref, cg_ref, din_hbm, kg_hbm,
     din_ref, kg_ref, img_ref, txt_ref, x_ref, g_ref, k_ref, bias_ref, gain_ref, terms_ref, xs, gs, ks, cs, ds, bs, load_sem,
-    ia, ta, ui, ut, vi, vt, probs, weights, flip, row_hi, row_lo, alpha, beta, row_all, col_all, gz, gx,
+    ia, ta, ui, ut, vi, vt, probs, weights, flip, pick, row_hi, row_lo, alpha, beta, row_raw, col_raw, row_all, col_all, gz, gx,
     zout, zin, xout, xin, yout, yin, l1, hsum, l2, qsum, l3, l4, fin,
     zag_s, zag_r, xag_s, xag_r, yag_s, yag_r, row_s, row_r, col_s, col_r,
     zrs_s, zrs_r, xrs_s, xrs_r, yrs_s, yrs_r,
@@ -232,6 +232,10 @@
         inverse[...] = inv
         everyone[full(index), :] = scaled.astype(bf16)
 
+    row_hi[...] = jnp.zeros_like(row_hi)
+    row_lo[...] = jnp.zeros_like(row_lo)
+    row_raw[...] = jnp.zeros_like(row_raw)
+    col_raw[...] = jnp.zeros_like(col_raw)
     loads[0].wait()
     unit_rows(txt_ref, ut, vt, ta, z)
     loads[1].wait()
@@ -250,20 +254,28 @@
         rows = slot(turn(z, -sign(d) * (k // 2 + 1), nz), (k % 2) ^ d)
         arrived(ta.at[rows], zag_s.at[d, k], zag_r.at[d, k])
 
-    def x_gather(q, d, k):
-        rows = slot((hy if q else yh) * nx + turn(x, -sign(d) * (k // 2), nx), (k % 2) ^ d)
+    def x_gather(part, d, s, facing_set=False):
+        side = hy if facing_set else yh
+        rows = slot(side * nx + turn(x, -sign(d) * s, nx), part)
         to = place(z, yh, turn(x, sign(d), nx))
-        start(ia.at[rows], ia.at[rows], xag_s.at[q, d, k], xag_r.at[q, d, k], to)
-
-    def x_gathered(q, d, k):
-        rows = slot((hy if q else yh) * nx + turn(x, -sign(d) * (k // 2 + 1), nx), (k % 2) ^ d)
-        arrived(ia.at[rows], xag_s.at[q, d, k], xag_r.at[q, d, k])
-
-    def y_gather(c):
-        start(ia.at[slot(b, c)], ia.at[slot(b, c)], yag_s.at[c], yag_r.at[c], facing)
-
-    def y_gathered(c):
-        arrived(ia.at[slot(hy * nx + x, c)], yag_s.at[c], yag_r.at[c])
+        i = 2 if facing_set else part
+        start(ia.at[rows], ia.at[rows], xag_s.at[i, d, s], xag_r.at[i, d, s], to)
+
+    def x_gathered(part, d, s, facing_set=False):
+        side = hy if facing_set else yh
+        rows = slot(side * nx + turn(x, -sign(d) * (s + 1), nx), part)
+        i = 2 if facing_set else part
+        arrived(ia.at[rows], xag_s.at[i, d, s], xag_r.at[i, d, s])
+
+    def y_gather(part, j):
+        rows = slot(yh * nx + turn(x, j, nx), part)
+        i = j + 1 if part else 0
+        start(ia.at[rows], ia.at[rows], yag_s.at[i], yag_r.at[i], facing)
+
+    def y_gathered(part, j):
+        rows = slot(hy * nx + turn(x, j, nx), part)
+        i = j + 1 if part else 0
+        arrived(ia.at[rows], yag_s.at[i], yag_r.at[i])
 
     def share(first, rows):
         return pl.ds(pl.multiple_of(first, 8), rows)
@@ -340,45 +352,49 @@
     def mate_spread_done():
         arrived(fin.at[share((geo.core - 1 - core) * geo.half, geo.half)], s7.at[0], r7.at[0])
 
-    half_scale = scale_ref[0] * 0.5
-    row_hi[...] = jnp.zeros_like(row_hi)
-    row_lo[...] = jnp.zeros_like(row_lo)
-    blocks = nz * ROWS // WIDE
-    late = turn(z, nz // 2, nz) // (WIDE // ROWS)
-
-    def logits_block(n):
-        lanes = pl.ds(pl.multiple_of(n * WIDE, WIDE), WIDE)
+    power = scale_ref[0] * (0.5 / math.log(2.0))
+    late = turn(z, nz // 2, nz)
+
+    def logits_block(tile, width, first, count, unroll=1):
+        lanes = pl.ds(pl.multiple_of(tile * ROWS, ROWS), width)
 
         def rows_step(m, sums):
-            rows = pl.ds(pl.multiple_of(m * WIDE, WIDE), WIDE)
+            rows = pl.ds(pl.multiple_of((first + m) * WIDE, WIDE), WIDE)
             logits = dot(ia[rows, :], ta[lanes, :], ((1,), (1,)))
-            root = jnp.exp(logits * half_scale)
+            root = jnp.exp2(logits * power)
             probs[rows, lanes] = root
             high = root * math.exp(-HIGH_SHIFT)
             high = high * high
             low = jnp.minimum(root * math.exp(LOW_SHIFT), math.exp(LOW_CAP))
             low = low * low
-            row_hi[rows, :] += high[:, :ROWS] + high[:, ROWS:]
-            row_lo[rows, :] += low[:, :ROWS] + low[:, ROWS:]
+            row_hi[rows, :] += sum(high[:, j : j + ROWS] for j in range(0, width, ROWS))
+            row_lo[rows, :] += sum(low[:, j : j + ROWS] for j in range(0, width, ROWS))
             return (
-                sums[0] + jnp.sum(high.reshape(WIDE // 8, 8, WIDE), axis=0),
-                sums[1] + jnp.sum(low.reshape(WIDE // 8, 8, WIDE), axis=0),
+                sums[0] + jnp.sum(high.reshape(WIDE // 8, 8, width), axis=0),
+                sums[1] + jnp.sum(low.reshape(WIDE // 8, 8, width), axis=0),
             )
 
-        zero = jnp.zeros((8, WIDE), f32)
-        high, low = lax.fori_loop(0, sheet * ROWS // WIDE, rows_step, (zero, zero))
+        zero = jnp.zeros((8, width), f32)
+        high, low = lax.fori_loop(0, count, rows_step, (zero, zero), unroll=unroll)
         high = jnp.sum(high, axis=0, keepdims=True)
         low = jnp.sum(low, axis=0, keepdims=True)
-        for j in range(WIDE // ROWS):
-            at = n * (WIDE // ROWS) + j
-            col_all[z, pl.ds(at, 1), :] = high[:, j * ROWS : (j + 1) * ROWS]
-            col_all[z, pl.ds(8 + at, 1), :] = low[:, j * ROWS : (j + 1) * ROWS]
-
-    def half_factor(total):
+        for j in range(width // ROWS):
+            col_raw[pl.ds(tile + j, 1), :] += high[:, j * ROWS : (j + 1) * ROWS]
+            col_raw[pl.ds(8 + tile + j, 1), :] += low[:, j * ROWS : (j + 1) * ROWS]
+
+    def local_lse(total):
         high, low = total[0:8], total[8:16]
         small = low < math.exp(LOW_LIMIT)
-        lse = jnp.where(small, jnp.log(low) - 2 * LOW_SHIFT, jnp.log(high) + 2 * HIGH_SHIFT)
-        return jnp.exp(lse * -0.5) * math.sqrt(0.5)
+        return jnp.where(small, jnp.log(low) - 2 * LOW_SHIFT, jnp.log(high) + 2 * HIGH_SHIFT)
+
+    def half_factor(parts, count):
+        peak = parts[0]
+        for o in range(1, count):
+            peak = jnp.maximum(peak, parts[o])
+        total = jnp.exp(parts[0] - peak)
+        for o in range(1, count):
+            total = total + jnp.exp(parts[o] - peak)
+        return jnp.exp((peak + jnp.log(total)) * -0.5) * math.sqrt(0.5)
 
     def weigh(tile):
         lanes = pl.ds(pl.multiple_of(tile * ROWS, ROWS), ROWS)
@@ -393,21 +409,21 @@
 
         lax.fori_loop(0, sheet * ROWS // WIDE, rows_step, 0)
 
-    def text_part(j):
-        flip[...] = weights[:, full(turn(z, j, nz))].T
-
-        @pl.loop(0, geo.width // WIDE)
-        def _(n):
-            lanes = pl.ds(pl.multiple_of(n * WIDE, WIDE), WIDE)
-            gz[j, :, lanes] = dot(flip[...], ia[:, lanes])
-
-    def image_part(q, j):
-        rows = full((yh if q else hy) * nx + turn(x, j, nx))
-
-        @pl.loop(0, geo.width // WIDE)
-        def _(n):
-            lanes = pl.ds(pl.multiple_of(n * WIDE, WIDE), WIDE)
-            gx[q * nx + j, :, lanes] = dot(weights[rows, :], ta[:, lanes])
+    def text_part(*shifts):
+        for i, j in enumerate(shifts):
+            flip[i * ROWS : (i + 1) * ROWS, :] = weights[:, full(turn(z, j, nz))].T
+        for n in range(0, geo.width, WIDE):
+            part = dot(flip[: len(shifts) * ROWS, :], ia[:, n : n + WIDE])
+            for i, j in enumerate(shifts):
+                gz[j, :, n : n + WIDE] = part[i * ROWS : (i + 1) * ROWS]
+
+    def image_part(*shifts):
+        for i, (q, j) in enumerate(shifts):
+            pick[i * ROWS : (i + 1) * ROWS, :] = weights[full((yh if q else hy) * nx + turn(x, j, nx)), :]
+        for n in range(0, geo.width, WIDE):
+            part = dot(pick[: len(shifts) * ROWS, :], ta[:, n : n + WIDE])
+            for i, (q, j) in enumerate(shifts):
+                gx[q * nx + j, :, n : n + WIDE] = part[i * ROWS : (i + 1) * ROWS]
 
     def ring_rows(d, k):
         part = (k % 2) ^ d
@@ -467,11 +483,11 @@
     for k in range(min(2, kz)):
         for d in both:
             z_gather(d, k)
-    for k in range(min(2, kx)):
+    for part in (1, 0):
         for d in both:
-            x_gather(0, d, k)
-    for c in both:
-        y_gather(c)
+            x_gather(part, d, 0)
+    y_gather(0, 0)
+    y_gather(1, 0)
     for load in loads[2:]:
         load.wait()
     conv_terms(x_ref, g_ref, k_ref, bias_ref, gain_ref, din_ref, terms_ref, xs, gs, ks, cs, ds, bs)
@@ -487,76 +503,78 @@
                 for d in both:
                     z_gather(d, k + 2)
 
-    def x_step(q, k):
-        if k < kx:
-            for d in both:
-                x_gathered(q, d, k)
-            if k + 2 < kx:
-                for d in both:
-                    x_gather(q, d, k + 2)
-
     z_step(0)
-    x_step(0, 0)
+    for d in both:
+        x_gathered(1, d, 0)
+    x_gather(1, 1, 1)
+    y_gather(1, nx - 1)
+    y_gather(1, 1)
+    y_gathered(0, 0)
+    for d in both:
+        x_gather(0, d, 0, True)
+    for d in both:
+        x_gathered(0, d, 0)
+    x_gather(0, 0, 1)
     z_step(1)
-    for c in both:
-        y_gathered(c)
-        for k in range(min(2, kx)):
-            for d in both:
-                if (k % 2) ^ d == c:
-                    x_gather(1, d, k)
     mate_sum()
     y_send()
-    x_step(0, 1)
+    x_gathered(1, 1, 1)
+    y_gather(1, 2)
+    pairs = nz * ROWS // WIDE
+    count = nx * ROWS // WIDE
+    lean = 2 * lax.rem(z, 2) - 1
+    near = 2 * (z // 2)
+    next_pair = 2 * turn(z // 2, lean, pairs)
+    far_pair = 2 * turn(z // 2, -lean, pairs)
+    ours, theirs = yh * count, hy * count
     z_step(2)
-    x_step(0, 2)
+    for d in both:
+        x_gathered(0, d, 0, True)
+    x_gather(0, 0, 1, True)
+    x_gathered(0, 0, 1)
+    logits_block(near, WIDE, ours, count)
+    z_step(3)
+    logits_block(next_pair, WIDE, ours, count)
+    for j in (0, nx - 1, 1):
+        y_gathered(1, j)
+    x_gathered(0, 0, 1, True)
+    z_step(4)
     y_sum()
     x_send()
-    z_step(3)
-    x_step(1, 0)
-    z_step(4)
-    x_sum()
-    for k in range(1, kx):
-        x_step(1, k)
+    y_gathered(1, 2)
+    logits_block(near, WIDE, theirs, count)
+    logits_block(next_pair, WIDE, theirs, count)
     for k in range(5, kz - 1):
         z_step(k)
-
-    @pl.loop(0, blocks - 1)
-    def _(i):
-        logits_block(lax.rem(late + 1 + i, blocks))
-
-    if kz - 1 >= 5:
-        z_step(kz - 1)
-    z_send()
-    logits_block(late)
+    x_sum()
+    logits_block(far_pair, WIDE, 0, 2 * count)
+    logits_block(late + 1 - 2 * lax.rem(late, 2), ROWS, 0, 2 * count)
+    z_step(kz - 1)
+    logits_block(late, ROWS, 0, 2 * count, True)
     for m in range(sheet):
         rows = slice(m * ROWS, (m + 1) * ROWS)
-        row_all[b, m : m + 1, :] = jnp.sum(row_hi[rows, :].T, axis=0, keepdims=True)
-        row_all[b, 8 + m : 9 + m, :] = jnp.sum(row_lo[rows, :].T, axis=0, keepdims=True)
-    for o in range(1, nz):
-        start(col_all.at[z], col_all.at[z], col_s.at[o], col_r.at[o], place(turn(z, o, nz), yh, x))
+        row_raw[m : m + 1, :] = jnp.sum(row_hi[rows, :].T, axis=0, keepdims=True)
+        row_raw[8 + m : 9 + m, :] = jnp.sum(row_lo[rows, :].T, axis=0, keepdims=True)
+    row_all[b] = local_lse(row_raw[...])
+    col_all[z] = local_lse(col_raw[...])
     for q in both:
         for o in range(nx):
             if q or o:
                 i = q * nx + o
                 to = place(z, hy if q else yh, turn(x, o, nx))
                 start(row_all.at[b], row_all.at[b], row_s.at[i], row_r.at[i], to)
-    z_sum()
-    x_spread()
+    for o in range(1, nz):
+        start(col_all.at[z], col_all.at[z], col_s.at[o], col_r.at[o], place(turn(z, o, nz), yh, x))
+    z_send()
     for o in range(1, nz):
         arrived(col_all.at[turn(z, -o, nz)], col_s.at[o], col_r.at[o])
-    total = col_all[0]
-    for o in range(1, nz):
-        total = total + col_all[o]
-    beta[...] = half_factor(total)
+    beta[...] = half_factor(col_all, nz)
     for q in both:
         for o in range(nx):
             if q or o:
                 i = q * nx + o
                 arrived(row_all.at[(hy if q else yh) * nx + turn(x, -o, nx)], row_s.at[i], row_r.at[i])
-    total = row_all[0]
-    for o in range(1, sheet):
-        total = total + row_all[o]
-    factor = half_factor(total)
+    factor = half_factor(row_all, sheet)
     for m in range(sheet):
         rows = slice(m * ROWS, (m + 1) * ROWS)
         alpha[rows, :] = jnp.broadcast_to(factor[m : m + 1, :], (ROWS, ROWS)).T
@@ -571,57 +589,44 @@
             for d in both:
                 x_reduce(q, d, k)
 
-    def text_parts(away):
-        if 0 < away < nz // 2:
-            text_part(away)
-            text_part(nz - away)
-
-    def image_parts(q, away):
-        if 0 < away < nx // 2:
-            image_part(q, away)
-            image_part(q, nx - away)
-
     half = nz // 2
     weigh(turn(z, half, nz))
     text_part(half)
     z_stage(0)
-    if half > 1:
-        weigh(turn(z, half - 1, nz))
-        weigh(turn(z, -(half - 1), nz))
-    text_parts(half - 1)
+
+    @pl.loop(0, nz - 1)
+    def _(i):
+        weigh(turn(z, i - (half - 1), nz))
+
+    image_part((0, 2))
+    x_stage(0, 0)
+    text_part(half - 1, nz - half + 1)
     z_stage(1)
-    first = max(half - 1, 1)
-
-    @pl.loop(0, 2 * first - 1)
-    def _(i):
-        weigh(turn(z, i - (first - 1), nz))
-
-    image_part(0, nx // 2)
-    x_stage(0, 0)
-    image_parts(0, nx // 2 - 1)
+    image_part((0, 1), (0, 3))
     x_stage(0, 1)
+    z_sum()
+    x_spread()
+    image_part((1, 2), (0, 0))
+    z_stage(2)
+    x_stage(0, 2)
+    x_stage(1, 0)
+    image_part((1, 1), (1, 3))
+    x_stage(1, 1)
+    text_part(half - 2, nz - half + 2)
+    z_stage(3)
     x_spread_done()
     y_spread()
-    image_part(1, nx // 2)
-    z_stage(2)
-    image_parts(1, nx // 2 - 1)
-    x_stage(0, 2)
-    x_stage(1, 0)
-    x_stage(1, 1)
-    text_parts(half - 2)
-    z_stage(3)
-    image_part(0, 0)
     z_stage(4)
     for c in both:
         yout[c] = x_total(0, c).astype(bf16)
         start(yout.at[c], yin.at[c], yrs_s.at[c], yrs_r.at[c], facing)
-    text_parts(half - 3)
+    text_part(half - 3, nz - half + 3)
     z_stage(5)
     x_stage(1, 2)
     y_spread_done()
     mate_spread()
     z_stage(6)
-    image_part(1, 0)
+    image_part((1, 0))
     text_part(0)
     mate_spread_done()
     for row in range(KS):
@@ -659,9 +664,10 @@
         big, big, big, big, big, vmem((2 * TILES, LANES), f32), dma((9,)),
         vmem((images, width), bf16), vmem((texts, width), bf16),
         vmem((ROWS, width), f32), vmem((ROWS, width), f32), vmem((ROWS, 1), f32), vmem((ROWS, 1), f32),
-        vmem((images, texts), f32), vmem((images, texts), bf16), vmem((ROWS, images), bf16),
+        vmem((images, texts), f32), vmem((images, texts), bf16), vmem((2 * ROWS, images), bf16), vmem((2 * ROWS, texts), bf16),
         vmem((images, ROWS), f32), vmem((images, ROWS), f32), vmem((images, ROWS), f32), vmem((8, ROWS), f32),
-        vmem((geo.sheet, 16, ROWS), f32), vmem((geo.z, 16, ROWS), f32),
+        vmem((16, ROWS), f32), vmem((16, ROWS), f32),
+        vmem((geo.sheet, 8, ROWS), f32), vmem((geo.z, 8, ROWS), f32),
         vmem((geo.z, ROWS, width), f32), vmem((2 * geo.x, ROWS, width), f32),
         vmem((2, kz, PART, width), bf16), vmem((2, kz, PART, width), bf16),
         vmem((2, 2, kx, PART, width), bf16), vmem((2, 2, kx, PART, width), bf16),
@@ -669,7 +675,7 @@
         vmem((geo.half, LANES), f32), vmem((geo.half, LANES), f32),
         vmem((geo.y, geo.y_rows, LANES), f32), vmem((geo.y_rows, LANES), f32),
         vmem((geo.x, geo.x_rows, LANES), f32), vmem((geo.z, geo.x_rows, LANES), f32), vmem((SLACK, LANES), f32),
-        dma((2, kz)), dma((2, kz)), dma((2, 2, kx)), dma((2, 2, kx)), dma((2,)), dma((2,)),
+        dma((2, kz)), dma((2, kz)), dma((3, 2, 2)), dma((3, 2, 2)), dma((1 + geo.x,)), dma((1 + geo.x,)),
         dma((geo.sheet,)), dma((geo.sheet,)), dma((geo.z,)), dma((geo.z,)),
         dma((2, kz)), dma((2, kz)), dma((2, 2, kx)), dma((2, 2, kx)), dma((2,)), dma((2,)),
         dma((1,)), dma((1,)), dma((geo.y,)), dma((geo.y,)), dma((geo.x,)), dma((geo.x,)), dma((geo.z,)), dma((geo.z,)),

time: 74.9 us -> 69.6 us (0.929)
  Pallas kernels: 73.4 us -> 68.1 us
    pallas_call x1, Pallas kernels: 71.1 us -> 65.8 us  [loss_block(): pl.pallas_call(functools.partial(loss_kernel, geo), out_shape=(jax.ShapeD...]
where the time goes in v5:
time: 69.6 us; the launch traced here: 69.4 us
  Pallas kernels  68.1 us (98%)
  between operations  1.29 us (2%)
    pallas_call x1, Pallas kernels, loss_block(): pl.pallas_call(functools.partial(loss_kernel, geo), out_shape=(jax.ShapeD...  65.8 us
    pallas_call x1, Pallas kernels, hand_out(): pl.pallas_call(hand_out_kernel, out_shape=tuple((jax.ShapeDtypeStruct(a.s...  2.32 us

profile of v5, /device:TPU:8, one launch (start us, length us, event | category | flops | bytes accessed | tf_op | source)
XLA Modules:
  0.0 69.4 jit_solution(8306005695647460851)
XLA Ops:
  1.3 65.8 %shard_map.119 = (bf16[128,1024]{1,0:T(8,128)(2,1)}, bf16[128,1024]{1,0:T(8,128)(2,1)}, f32[3,3072]{1,0:T(4,128)}, bf16[7,7,3072]{2,1,0:T(8,128)(2,1)}, f32[7,7,3072]{2,1,0:T(8,128)}) custom-call(f32[1]{0:T(128)} %bitcast.8.scale_ref, bf16[128,1024]{1,0:T(8,128)(2,1)} %bitcast.11, bf16[128,1024]{1,0:T(8,128)(2,1)} %bitcast.12, bf16[7,7,3072]{2,1,0:T(8,128)(2,1)} %bitcast.9, ...), custom_call_target="tpu_custom_call" | custom-call | tf_op jit(solution)/shard_map/pallas_call | solution.py:684
  67.1 2.3 %shard_map.120 = (bf16[128,1024]{1,0:T(8,128)(2,1)}, bf16[128,1024]{1,0:T(8,128)(2,1)}, f32[3,3072]{1,0:T(4,128)}, bf16[7,7,3072]{2,1,0:T(8,128)(2,1)}, f32[7,7,3072]{2,1,0:T(8,128)}) custom-call(bf16[128,1024]{1,0:T(8,128)(2,1)} %get-tuple-element.15.refs_0_, bf16[128,1024]{1,0:T(8,128)(2,1)} %get-tuple-element.16.refs_1_, ...), custom_call_target="tpu_custom_call" | custom-call | tf_op jit(solution)/shard_map/pallas_call | solution.py:719

commit v6 on v5

--- a/solution.py
+++ b/solution.py
@@ -199,14 +199,9 @@
         copy(dst, dst, send, recv, facing).wait_recv()
 
     barrier = pltpu.get_barrier_semaphore()
-    peers = [place(turn(z, o, nz), yh, x) for o in range(1, nz)]
-    for q in range(2):
-        for o in range(nx):
-            if q or o:
-                peers.append(place(z, hy if q else yh, turn(x, o, nx)))
-    for o in range(1, geo.y):
-        if o != geo.y_lo:
-            peers.append(column(turn(y, o, geo.y)))
+    peers = [place(turn(z, o, nz), yh, x) for o in (-1, 1)]
+    peers += [place(z, yh, turn(x, o, nx)) for o in (-1, 1)]
+    peers += [column(turn(y, o, geo.y)) for o in range(1, geo.y)]
     peers.append(mate)
     for peer in peers:
         pl.semaphore_signal(barrier, inc=1, device_id=peer, device_id_type=MESH)

time: 69.6 us -> 68.6 us (0.986); the launches traced: 69.4 us -> 67.7 us
  Pallas kernels: 68.1 us -> 66.4 us
    pallas_call x1, Pallas kernels: 65.8 us -> 64.1 us  [loss_block(): pl.pallas_call(functools.partial(loss_kernel, geo), out_shape=(jax.ShapeD...]
where the time goes in v6:
time: 68.6 us; the launch traced here: 67.7 us
  Pallas kernels  66.4 us (97%)
  between operations  1.29 us (2%)
    pallas_call x1, Pallas kernels, loss_block(): pl.pallas_call(functools.partial(loss_kernel, geo), out_shape=(jax.ShapeD...  64.1 us
    pallas_call x1, Pallas kernels, hand_out(): pl.pallas_call(hand_out_kernel, out_shape=tuple((jax.ShapeDtypeStruct(a.s...  2.32 us

profile of v6, /device:TPU:8, one launch (start us, length us, event | category | flops | bytes accessed | tf_op | source)
XLA Modules:
  0.0 67.7 jit_solution(8336600209264565191)
XLA Ops:
  1.3 64.1 %shard_map.119 = (bf16[128,1024]{1,0:T(8,128)(2,1)}, bf16[128,1024]{1,0:T(8,128)(2,1)}, f32[3,3072]{1,0:T(4,128)}, bf16[7,7,3072]{2,1,0:T(8,128)(2,1)}, f32[7,7,3072]{2,1,0:T(8,128)}) custom-call(f32[1]{0:T(128)} %bitcast.8.scale_ref, bf16[128,1024]{1,0:T(8,128)(2,1)} %bitcast.11, bf16[128,1024]{1,0:T(8,128)(2,1)} %bitcast.12, bf16[7,7,3072]{2,1,0:T(8,128)(2,1)} %bitcast.9, ...), custom_call_target="tpu_custom_call" | custom-call | tf_op jit(solution)/shard_map/pallas_call | solution.py:679
  65.4 2.3 %shard_map.120 = (bf16[128,1024]{1,0:T(8,128)(2,1)}, bf16[128,1024]{1,0:T(8,128)(2,1)}, f32[3,3072]{1,0:T(4,128)}, bf16[7,7,3072]{2,1,0:T(8,128)(2,1)}, f32[7,7,3072]{2,1,0:T(8,128)}) custom-call(bf16[128,1024]{1,0:T(8,128)(2,1)} %get-tuple-element.15.refs_0_, bf16[128,1024]{1,0:T(8,128)(2,1)} %get-tuple-element.16.refs_1_, ...), custom_call_target="tpu_custom_call" | custom-call | tf_op jit(solution)/shard_map/pallas_call | solution.py:714

commit v7 on v6

--- a/solution.py
+++ b/solution.py
@@ -437,8 +437,19 @@
         to = place(turn(z, sign(d), nz), yh, x)
         start(zout.at[d, k], zin.at[d, k], zrs_s.at[d, k], zrs_r.at[d, k], to)
 
+    def y_early(j):
+        yout[1 + j] = gx[j, PART:, :].astype(bf16)
+        start(yout.at[1 + j], yin.at[1 + j], yrs_s.at[1 + j], yrs_r.at[1 + j], facing)
+
+    def y_arrived(i):
+        arrived(yin.at[i], yrs_s.at[i], yrs_r.at[i])
+        return yin[i].astype(f32)
+
     def x_reduce(q, d, k):
-        value = gx[q * nx + ring_target(d, k, nx), ring_rows(d, k), :]
+        target = ring_target(d, k, nx)
+        value = gx[q * nx + target, ring_rows(d, k), :]
+        if (k % 2) ^ d == 1:
+            value = value + y_arrived(1 + target)
         if k >= 2:
             arrived(xin.at[q, d, k - 2], xrs_s.at[q, d, k - 2], xrs_r.at[q, d, k - 2])
             value = value + xin[q, d, k - 2].astype(f32)
@@ -579,11 +590,6 @@
             for d in both:
                 z_reduce(d, k)
 
-    def x_stage(q, k):
-        if k < kx:
-            for d in both:
-                x_reduce(q, d, k)
-
     half = nz // 2
     weigh(turn(z, half, nz))
     text_part(half)
@@ -593,35 +599,40 @@
     def _(i):
         weigh(turn(z, i - (half - 1), nz))
 
-    image_part((0, 2))
-    x_stage(0, 0)
+    image_part((0, 2), (0, 3))
+    x_reduce(0, 0, 0)
+    x_reduce(0, 1, 1)
+    y_early(2)
+    y_early(3)
     text_part(half - 1, nz - half + 1)
     z_stage(1)
-    image_part((0, 1), (0, 3))
-    x_stage(0, 1)
     z_sum()
     x_spread()
-    image_part((1, 2), (0, 0))
+    image_part((0, 1), (0, 0))
+    y_early(1)
+    image_part((1, 2), (1, 3))
+    x_reduce(1, 0, 0)
+    x_reduce(1, 1, 1)
     z_stage(2)
-    x_stage(0, 2)
-    x_stage(1, 0)
-    image_part((1, 1), (1, 3))
-    x_stage(1, 1)
+    x_reduce(0, 0, 2)
+    image_part((1, 1), (1, 0))
+    x_spread_done()
+    y_spread()
+    x_reduce(1, 1, 0)
     text_part(half - 2, nz - half + 2)
     z_stage(3)
-    x_spread_done()
-    y_spread()
+    x_reduce(1, 0, 2)
     z_stage(4)
-    for c in both:
-        yout[c] = x_total(0, c).astype(bf16)
-        start(yout.at[c], yin.at[c], yrs_s.at[c], yrs_r.at[c], facing)
+    x_reduce(1, 0, 1)
+    yout[0] = x_total(0, 0).astype(bf16)
+    start(yout.at[0], yin.at[0], yrs_s.at[0], yrs_r.at[0], facing)
+    y_early(0)
     text_part(half - 3, nz - half + 3)
     z_stage(5)
-    x_stage(1, 2)
+    x_reduce(1, 1, 2)
     y_spread_done()
     mate_spread()
     z_stage(6)
-    image_part((1, 0))
     text_part(0)
     mate_spread_done()
     for row in range(KS):
@@ -634,9 +645,8 @@
     kg_out = pltpu.make_async_copy(kg_ref, kg_hbm, load_sem.at[len(loads) + 1])
     kg_out.start()
     for c in both:
-        value = x_total(1, c)
-        arrived(yin.at[c], yrs_s.at[c], yrs_r.at[c])
-        finish(value + yin[c].astype(f32), ta[slot(z, c), :], ui, vi, ig_ref, c)
+        value = x_total(1, c) + y_arrived(c)
+        finish(value, ta[slot(z, c), :], ui, vi, ig_ref, c)
     for c in both:
         finish(z_total(c), ia[slot(b, c), :], ut, vt, tg_ref, c)
     din_out.wait()
@@ -651,7 +661,7 @@
     dma = pltpu.SemaphoreType.DMA
     images, texts, width = geo.sheet * ROWS, geo.z * ROWS, geo.width
     kz, kx = geo.z - 1, geo.x - 1
-    big = vmem((SPOTS * TILES, LANES), f32)
+    big = vmem((SPOTS * TILES + TILES, LANES), f32)
     maps = vmem((GRID, GRID, TILES * LANES), bf16)
     scratch = [
         maps, vmem((KS, KS, TILES * LANES), f32), vmem((ROWS, width), bf16), vmem((ROWS, width), bf16), maps, maps, maps,
@@ -666,13 +676,13 @@
         vmem((geo.z, ROWS, width), f32), vmem((2 * geo.x, ROWS, width), f32),
         vmem((2, kz, PART, width), bf16), vmem((2, kz, PART, width), bf16),
         vmem((2, 2, kx, PART, width), bf16), vmem((2, 2, kx, PART, width), bf16),
-        vmem((2, PART, width), bf16), vmem((2, PART, width), bf16),
+        vmem((1 + geo.x, PART, width), bf16), vmem((1 + geo.x, PART, width), bf16),
         vmem((geo.half, LANES), f32), vmem((geo.half, LANES), f32),
         vmem((geo.y, geo.y_rows, LANES), f32), vmem((geo.y_rows, LANES), f32),
         vmem((geo.x, geo.x_rows, LANES), f32), vmem((geo.z, geo.x_rows, LANES), f32), vmem((SLACK, LANES), f32),
         dma((2, kz)), dma((2, kz)), dma((3, 2, 2)), dma((3, 2, 2)), dma((1 + geo.x,)), dma((1 + geo.x,)),
         dma((geo.sheet,)), dma((geo.sheet,)), dma((geo.z,)), dma((geo.z,)),
-        dma((2, kz)), dma((2, kz)), dma((2, 2, kx)), dma((2, 2, kx)), dma((2,)), dma((2,)),
+        dma((2, kz)), dma((2, kz)), dma((2, 2, kx)), dma((2, 2, kx)), dma((1 + geo.x,)), dma((1 + geo.x,)),
         dma((1,)), dma((1,)), dma((geo.y,)), dma((geo.y,)), dma((geo.x,)), dma((geo.x,)), dma((geo.z,)), dma((geo.z,)),
         dma((geo.x,)), dma((geo.x,)), dma((geo.y,)), dma((geo.y,)), dma((1,)), dma((1,)),
     ]

time: 68.6 us -> 67.7 us (0.987)
  no operation moved by 1% of the time
where the time goes in v7:
time: 67.7 us; the launch traced here: 67.5 us
  Pallas kernels  66.2 us (98%)
  between operations  1.29 us (2%)
    pallas_call x1, Pallas kernels, loss_block(): pl.pallas_call(functools.partial(loss_kernel, geo), out_shape=(jax.ShapeD...  63.9 us
    pallas_call x1, Pallas kernels, hand_out(): pl.pallas_call(hand_out_kernel, out_shape=tuple((jax.ShapeDtypeStruct(a.s...  2.32 us

profile of v7, /device:TPU:8, one launch (start us, length us, event | category | flops | bytes accessed | tf_op | source)
XLA Modules:
  0.0 67.5 jit_solution(1469658291550633850)
XLA Ops:
  1.3 63.9 %shard_map.119 = (bf16[128,1024]{1,0:T(8,128)(2,1)}, bf16[128,1024]{1,0:T(8,128)(2,1)}, f32[3,3072]{1,0:T(4,128)}, bf16[7,7,3072]{2,1,0:T(8,128)(2,1)}, f32[7,7,3072]{2,1,0:T(8,128)}) custom-call(f32[1]{0:T(128)} %bitcast.8.scale_ref, bf16[128,1024]{1,0:T(8,128)(2,1)} %bitcast.11, bf16[128,1024]{1,0:T(8,128)(2,1)} %bitcast.12, bf16[7,7,3072]{2,1,0:T(8,128)(2,1)} %bitcast.9, ...), custom_call_target="tpu_custom_call" | custom-call | tf_op jit(solution)/shard_map/pallas_call | solution.py:689
  65.1 2.3 %shard_map.120 = (bf16[128,1024]{1,0:T(8,128)(2,1)}, bf16[128,1024]{1,0:T(8,128)(2,1)}, f32[3,3072]{1,0:T(4,128)}, bf16[7,7,3072]{2,1,0:T(8,128)(2,1)}, f32[7,7,3072]{2,1,0:T(8,128)}) custom-call(bf16[128,1024]{1,0:T(8,128)(2,1)} %get-tuple-element.15.refs_0_, bf16[128,1024]{1,0:T(8,128)(2,1)} %get-tuple-element.16.refs_1_, ...), custom_call_target="tpu_custom_call" | custom-call | tf_op jit(solution)/shard_map/pallas_call | solution.py:724

commit v8 on v7

--- a/solution.py
+++ b/solution.py
@@ -152,7 +152,7 @@
 
 def loss_kernel(
     geo, scale_ref, img_hbm, txt_hbm, x_hbm, g_hbm, k_hbm, bias_hbm, gain_hbm,
-    ig_ref, tg_ref, cg_ref, din_hbm, kg_hbm,
+    ig_hbm, tg_hbm, cg_hbm, din_hbm, kg_hbm, ig_ref, tg_ref, cg_ref,
     din_ref, kg_ref, img_ref, txt_ref, x_ref, g_ref, k_ref, bias_ref, gain_ref, terms_ref, xs, gs, ks, cs, ds, bs, load_sem,
     ia, ta, ui, ut, vi, vt, probs, weights, flip, pick, row_hi, row_lo, alpha, beta, row_raw, col_raw, row_all, col_all, gz, gx,
     zout, zin, xout, xin, yout, yin, l1, hsum, l2, qsum, l3, l4, fin,
@@ -644,15 +644,23 @@
         cg_ref[:, t * LANES : (t + 1) * LANES] = fin[pl.ds(SPOTS * TILES + t, 3, stride=TILES), :]
     kg_out = pltpu.make_async_copy(kg_ref, kg_hbm, load_sem.at[len(loads) + 1])
     kg_out.start()
+    cg_out = pltpu.make_async_copy(cg_ref, cg_hbm, load_sem.at[len(loads) + 2])
+    cg_out.start()
     for c in both:
         value = x_total(1, c) + y_arrived(c)
         finish(value, ta[slot(z, c), :], ui, vi, ig_ref, c)
+    ig_out = pltpu.make_async_copy(ig_ref, ig_hbm, load_sem.at[len(loads) + 3])
+    ig_out.start()
+    tg_out = []
     for c in both:
         finish(z_total(c), ia[slot(b, c), :], ut, vt, tg_ref, c)
-    din_out.wait()
-    kg_out.wait()
+        rows = pl.ds(c * PART, PART)
+        tg_out.append(pltpu.make_async_copy(tg_ref.at[rows], tg_hbm.at[rows], load_sem.at[len(loads) + 4 + c]))
+        tg_out[c].start()
     for moving in sent:
         moving.wait_send()
+    for leaving in (din_out, kg_out, cg_out, ig_out, *tg_out):
+        leaving.wait()
 
 
 def loss_block(geo, scale, image_rows, text_rows, x, g, k, bias, gain):
@@ -664,9 +672,10 @@
     big = vmem((SPOTS * TILES + TILES, LANES), f32)
     maps = vmem((GRID, GRID, TILES * LANES), bf16)
     scratch = [
+        vmem((ROWS, width), bf16), vmem((ROWS, width), bf16), vmem((3, TILES * LANES), f32),
         maps, vmem((KS, KS, TILES * LANES), f32), vmem((ROWS, width), bf16), vmem((ROWS, width), bf16), maps, maps, maps,
         vmem((TILES * LANES,), bf16), vmem((TILES * LANES,), bf16), vmem((SLACK, LANES), f32),
-        big, big, big, big, big, vmem((2 * TILES, LANES), f32), dma((9,)),
+        big, big, big, big, big, vmem((2 * TILES, LANES), f32), dma((13,)),
         vmem((images, width), bf16), vmem((texts, width), bf16),
         vmem((ROWS, width), f32), vmem((ROWS, width), f32), vmem((ROWS, 1), f32), vmem((ROWS, 1), f32),
         vmem((images, texts), f32), vmem((images, texts), bf16), vmem((2 * ROWS, images), bf16), vmem((2 * ROWS, texts), bf16),
@@ -696,7 +705,7 @@
             jax.ShapeDtypeStruct((KS, KS, TILES * LANES), f32),
         ),
         in_specs=[pl.BlockSpec(memory_space=pltpu.SMEM)] + [pl.BlockSpec(memory_space=pltpu.HBM)] * 7,
-        out_specs=[pl.BlockSpec(memory_space=pltpu.VMEM)] * 3 + [pl.BlockSpec(memory_space=pltpu.HBM)] * 2,
+        out_specs=[pl.BlockSpec(memory_space=pltpu.HBM)] * 5,
         scratch_shapes=scratch,
         compiler_params=pltpu.CompilerParams(
             collective_id=0, has_side_effects=True, vmem_limit_bytes=60 << 20

time: 67.7 us -> 67.4 us (level)
  no operation moved by 1% of the time
where the time goes in v8:
time: 67.4 us; the launch traced here: 67.2 us
  Pallas kernels  65.9 us (98%)
  between operations  1.29 us (2%)
    pallas_call x1, Pallas kernels, loss_block(): pl.pallas_call(functools.partial(loss_kernel, geo), out_shape=(jax.ShapeD...  63.6 us
    pallas_call x1, Pallas kernels, hand_out(): pl.pallas_call(hand_out_kernel, out_shape=tuple((jax.ShapeDtypeStruct(a.s...  2.32 us

profile of v8, /device:TPU:8, one launch (start us, length us, event | category | flops | bytes accessed | tf_op | source)
XLA Modules:
  0.0 67.2 jit_solution(3634925951211717317)
XLA Ops:
  1.3 63.6 %shard_map.119 = (bf16[128,1024]{1,0:T(8,128)(2,1)}, bf16[128,1024]{1,0:T(8,128)(2,1)}, f32[3,3072]{1,0:T(4,128)}, bf16[7,7,3072]{2,1,0:T(8,128)(2,1)}, f32[7,7,3072]{2,1,0:T(8,128)}) custom-call(f32[1]{0:T(128)} %bitcast.8.scale_ref, bf16[128,1024]{1,0:T(8,128)(2,1)} %bitcast.11, bf16[128,1024]{1,0:T(8,128)(2,1)} %bitcast.12, bf16[7,7,3072]{2,1,0:T(8,128)(2,1)} %bitcast.9, ...), custom_call_target="tpu_custom_call" | custom-call | tf_op jit(solution)/shard_map/pallas_call | solution.py:698
  64.9 2.3 %shard_map.120 = (bf16[128,1024]{1,0:T(8,128)(2,1)}, bf16[128,1024]{1,0:T(8,128)(2,1)}, f32[3,3072]{1,0:T(4,128)}, bf16[7,7,3072]{2,1,0:T(8,128)(2,1)}, f32[7,7,3072]{2,1,0:T(8,128)}) custom-call(bf16[128,1024]{1,0:T(8,128)(2,1)} %get-tuple-element.15.refs_0_, bf16[128,1024]{1,0:T(8,128)(2,1)} %get-tuple-element.16.refs_1_, ...), custom_call_target="tpu_custom_call" | custom-call | tf_op jit(solution)/shard_map/pallas_call | solution.py:733
